TPU v7x, 32 devices: a whole 2x2x4 slice. The times are simulated.
32 devices in a mesh: cells: 8 (over z, y), per: 4 (over x, core).
Axes of the slice: x: 2, y: 2, z: 4, core: 2. Of those that a mesh axis runs over, the one named last changes fastest.
Arguments:
- field: float32 [128, 2, 8, 4096], P('per', None, None, 'cells'), may hold values from -12 to 12
- period_gain: float32 [128], replicated, may hold values from 0.3 to 3
- start_basis: float32 [128, 32], replicated, may hold values from -0.5 to 0.5
Outputs:
- projected: float32 [128, 2, 8, 4096], P('per', None, None, 'cells')
All inputs are finite; a program needn't handle non-finite values.
Results may differ from a plain program's by a relative error of at most 0.0003.
Values sent between devices are 32-bit elements; how exact they have to be, the bound alone decides.
A program may use at most 192 MiB of HBM per device.

v0:
```python
import jax
import jax.numpy as jnp
from jax import lax
from jax.sharding import PartitionSpec as P

ITERS = 3


HIGH = lax.Precision.HIGHEST


def refine(gram, basis):
    for step in range(ITERS):
        grown = jnp.dot(gram, basis, precision=HIGH)
        inner = jnp.dot(grown.T, grown, precision=HIGH)
        lower = jnp.linalg.cholesky(inner)
        basis = lax.linalg.triangular_solve(
            lower, grown, left_side=False, lower=True, transpose_a=True
        )
    return basis


def per_device(field, period_gain, start_basis):
    group_index = lax.axis_index("per")
    local_periods = field.shape[0]
    gains = lax.dynamic_slice_in_dim(period_gain, group_index * local_periods, local_periods)
    scaled = field * gains[:, None, None, None]
    total_rows = 2.0 * field.shape[2] * field.shape[3] * lax.axis_size("cells")
    rows = lax.all_to_all(scaled, "per", split_axis=2, concat_axis=0, tiled=True)
    flat = rows.reshape(rows.shape[0], -1)
    local_gram = lax.dot_general(flat, flat, (((1,), (1,)), ((), ())), precision=HIGH) / total_rows
    gram = lax.psum(local_gram, ("cells", "per"))
    basis = refine(gram, start_basis)
    projector = jnp.dot(basis, basis.T, precision=HIGH)
    result = lax.dot_general(projector, flat, (((0,), (0,)), ((), ())), precision=HIGH)
    result = result.reshape(rows.shape)
    return lax.all_to_all(result, "per", split_axis=0, concat_axis=2, tiled=True)


def solution(mesh):
    in_specs = (P("per", None, None, "cells"), P(), P())
    out_specs = P("per", None, None, "cells")
    return jax.shard_map(
        per_device, mesh=mesh, in_specs=in_specs, out_specs=out_specs, check_vma=False
    )
```

profile of v0, /device:TPU:0, one launch (start us, length us, event | category | flops | bytes accessed | tf_op | source)
XLA Modules:
  0.0 201.5 jit_solution(17861391906963616649)
XLA Ops:
  6.5 0.0 copy-start
  6.5 0.0 all-reduce.2.cloned.1.call-start
  6.5 0.0 copy-start.2
  6.5 0.7 copy-done.2
  7.2 0.1 dynamic_slice.3
  7.3 1.8 copy_multiply_fusion
  9.1 18.5 %all_to_all.33 = f32[32,2,8,512]{3,0,1,2:T(8,128)S(1)} all-to-all(f32[32,2,8,512]{3,0,1,2:T(8,128)S(1)} %copy_multiply_fusion), channel_id=1, replica_groups=mesh['cells'=8,'per'=4] {'per'}, dimensions={2} | all-to-all | bytes 2097152 | tf_op jit(solution)/shard_map/all_to_all | solution.py:29
  27.6 0.8 copy.37
  28.4 0.9 reshape.18
  29.3 1.6 convolution_multiply_fusion
  30.9 0.0 all-reduce.2.cloned.1.call-update
  31.0 0.3 copy.29
  31.3 117.7 %all-reduce.2.cloned.1.call-done = f32[128,128]{1,0:T(8,128)} async-done(((f32[128,128]{1,0:T(8,128)}), f32[128,128]{1,0:T(8,128)}) %all-reduce.2.cloned.1.call-update) | async-done | bytes 65552 | tf_op jit(solution)/shard_map/psum | solution.py:32
  149.0 0.0 copy-done
  149.0 1.0 fusion.13
  150.0 0.2 fusion.14
  150.2 0.1 copy.26
  150.3 0.0 copy-start.1
  150.3 2.9 %cholesky.59 = f32[32,32]{1,0:T(8,128)S(1)} custom-call(f32[32,32]{1,0:T(8,128)S(1)} %fusion.8), custom_call_target="Cholesky" | custom-call | tf_op jit(solution)/shard_map/jit(cholesky)/cholesky | solution.py:16
  153.2 0.6 compare_reduce_fusion.2
  153.9 0.7 fusion
  154.5 2.4 %custom-call.7 = f32[1,32,32]{1,2,0:T(8,128)S(1)} custom-call(f32[1,32,32]{2,1,0:T(8,128)S(1)} %fusion), custom_call_target="InvertDiagBlocksLowerTriangular" | custom-call | tf_op jit(solution)/shard_map/triangular_solve/custom-call.0 | solution.py:17
  157.0 0.2 convolution_bitcast_fusion.3
  157.2 0.0 copy-done.1
  157.2 0.2 fusion.15
  157.4 0.2 fusion.16
  157.6 0.1 copy.27
  157.7 2.9 %cholesky.70 = f32[32,32]{1,0:T(8,128)S(1)} custom-call(f32[32,32]{1,0:T(8,128)S(1)} %fusion.6), custom_call_target="Cholesky" | custom-call | tf_op jit(solution)/shard_map/jit(cholesky)/cholesky | solution.py:16
  160.6 0.6 compare_reduce_fusion.1
  161.3 0.7 fusion.1
  161.9 2.4 %custom-call.8 = f32[1,32,32]{1,2,0:T(8,128)S(1)} custom-call(f32[1,32,32]{2,1,0:T(8,128)S(1)} %fusion.1), custom_call_target="InvertDiagBlocksLowerTriangular" | custom-call | tf_op jit(solution)/shard_map/triangular_solve/custom-call.0 | solution.py:17
  164.4 0.2 convolution_bitcast_fusion.2
  164.6 0.2 fusion.17
  164.8 0.2 fusion.18
  165.0 0.1 copy.28
  165.1 2.9 %cholesky.81 = f32[32,32]{1,0:T(8,128)S(1)} custom-call(f32[32,32]{1,0:T(8,128)S(1)} %fusion.4), custom_call_target="Cholesky" | custom-call | tf_op jit(solution)/shard_map/jit(cholesky)/cholesky | solution.py:16
  168.0 0.6 compare_reduce_fusion
  168.7 0.7 fusion.2
  169.3 2.4 %custom-call.9 = f32[1,32,32]{1,2,0:T(8,128)S(1)} custom-call(f32[1,32,32]{2,1,0:T(8,128)S(1)} %fusion.2), custom_call_target="InvertDiagBlocksLowerTriangular" | custom-call | tf_op jit(solution)/shard_map/triangular_solve/custom-call.0 | solution.py:17
  171.8 0.2 convolution_bitcast_fusion.1
  172.0 0.3 convolution_bitcast_fusion
  172.3 1.0 fusion.19
  173.4 0.8 copy.31
  174.2 18.2 %all_to_all.34 = f32[128,2,2,512]{3,2,1,0:T(2,128)S(1)} all-to-all(f32[128,2,2,512]{3,2,1,0:T(2,128)S(1)} %copy.31), channel_id=1, replica_groups=mesh['cells'=8,'per'=4] {'per'}, dimensions={0} | all-to-all | bytes 2097152 | tf_op jit(solution)/shard_map/all_to_all | solution.py:37
  192.4 0.6 copy.32
  193.0 1.7 all_to_all.30
  (6 shorter events, 0.1 us)
Async XLA Ops:
  6.5 142.4 %copy-start = (f32[128,32]{0,1:T(8,128)S(1)}, f32[128,32]{0,1:T(8,128)}, u32[]{:S(2)}) copy-start(f32[128,32]{0,1:T(8,128)} %param.8) | copy-start | bytes 49156
  6.5 142.4 %all-reduce.2.cloned.1.call-start = ((), (), s32[]{:S(2)}) async-start(), calls=%async_computation.2 | async-start | bytes 131072 | tf_op jit(solution)/shard_map/psum | solution.py:32
  6.5 0.7 copy-start.2
  150.3 7.0 %copy-start.1 = (f32[128,128]{1,0:T(8,128)S(1)}, f32[128,128]{1,0:T(8,128)}, u32[]{:S(2)}) copy-start(f32[128,128]{1,0:T(8,128)} %all-reduce.2.cloned.1.call-done) | copy-start | bytes 196612
Sparse Core Ops, SparseCore 0:
  31.1 117.8 all-reduce.1
where the time goes:
time: 202 us
  waiting for transfers between devices  118 us (58%)
  blocking collectives  36.7 us (18%)
  other arithmetic  21.9 us (11%)
  between operations  13.6 us (7%)
  local copies, waits for them, and re-layouts  6.11 us (3%)
  matrix products  5.55 us (3%)
    psum x1, waiting for transfers between devices, per_device(): gram = lax.psum(local_gram, ('cells', 'per'))  118 us
    all_to_all x1, blocking collectives, per_device(): lax.all_to_all(scaled, 'per', split_axis=2, concat_axis=0, tiled=True)  18.5 us
    all_to_all x1, blocking collectives, per_device(): lax.all_to_all(result, 'per', split_axis=0, concat_axis=2, tiled=True)  18.2 us
    another operation x9, other arithmetic, refine(): lower = jnp.linalg.cholesky(inner)  10.8 us
    another operation x6, other arithmetic, refine(): lax.linalg.triangular_solve(lower, grown, left_side=False, lower=True, tr...  9.26 us
  transfers between devices with their start and end apart: 1, of which 1 were waited for; matrix products, arithmetic and copies ran while one was open for 0% of the time, Pallas kernels for 0%

commit v1 on v0

v1 whole, which is shorter than its diff:
```python
import functools
import jax
import jax.numpy as jnp
from jax import lax
from jax.experimental import pallas as pl
from jax.experimental.pallas import tpu as pltpu
from jax.sharding import PartitionSpec as P

ITERS = 3
HIGH = lax.Precision.HIGHEST
MESH = pl.DeviceIdType.MESH
F32 = jnp.float32
BF16 = jnp.bfloat16


def split_two(x):
    hi = x.astype(BF16)
    return hi, (x - hi.astype(F32)).astype(BF16)


def refine_step(gram, basis_t):
    rank, periods = basis_t.shape
    grown = jnp.dot(basis_t, gram, precision=HIGH, preferred_element_type=F32)
    inner = lax.dot_general(grown, grown, (((1,), (1,)), ((), ())), precision=HIGH,
                            preferred_element_type=F32)
    row_id = lax.broadcasted_iota(jnp.int32, (rank, 1), 0)
    for k in range(rank - 1):
        below = jnp.where(row_id > k, inner[:, k:k + 1], 0.0)
        inverse = 1.0 / inner[k:k + 1, k:k + 1]
        grown_row = grown[k:k + 1, :] * inverse
        inner_row = inner[k:k + 1, :] * inverse
        grown = grown - below * grown_row
        inner = inner - below * inner_row
    eye = lax.broadcasted_iota(jnp.int32, (rank, rank), 0) == lax.broadcasted_iota(
        jnp.int32, (rank, rank), 1)
    pivots = jnp.sum(jnp.where(eye, inner, 0.0), axis=1, keepdims=True)
    return grown * lax.rsqrt(pivots)


def kernel(cells, total_rows, field, gain_ref, start_ref, out, buf, parts, out_buf, gram_part,
           scattered, slots, gram_full, proj_ref, local_sem, out_sem, send1, recv1, send2, recv2,
           relay_send, relay_recv, rs_send, rs_recv, bc_send, bc_recv, ag_send, ag_recv):
    me = lax.axis_index("per")
    my_cell = lax.axis_index("cells")
    sib = me + 1 - 2 * lax.rem(me, 2)
    peer = lax.rem(me + 2, 4)
    cross = lax.rem(sib + 2, 4)
    base = 2 * (1 - me // 2)
    others = (sib, peer, cross)
    own = field.shape[0]
    layers = field.shape[2]
    rows = 2 * layers

    def lanes(j):
        return pl.ds(pl.multiple_of(j * 128, 128), 128)

    local = []
    for index, j in enumerate((me,) + others):
        copy = pltpu.make_async_copy(field.at[:, :, :, lanes(j)], buf.at[j, me], local_sem.at[index])
        copy.start()
        local.append(copy)

    barrier = pltpu.get_barrier_semaphore()
    for other in others:
        pl.semaphore_signal(barrier, inc=1, device_id={"per": other}, device_id_type=MESH)

    def greet(step, carry):
        pl.semaphore_signal(barrier, inc=1, device_id={"cells": lax.rem(my_cell + step, cells)},
                            device_id_type=MESH)
        return carry

    lax.fori_loop(1, cells, greet, 0)
    pl.semaphore_wait(barrier, 3 + cells - 1)

    def remote(src, dst, send, recv, other):
        return pltpu.make_async_remote_copy(src_ref=src, dst_ref=dst, send_sem=send, recv_sem=recv,
                                            device_id={"per": other}, device_id_type=MESH)

    first = {}
    for a in range(2):
        for rel in (1, 2, 0):
            other = others[rel]
            copy = remote(field.at[:, a, :, lanes(other)], buf.at[other, me, :, a],
                          send1.at[rel, a], recv1.at[rel, a], other)
            copy.start()
            first[rel, a] = copy

    second = []
    for index, j in enumerate((me, peer, cross)):
        copy = remote(field.at[:, :, :, lanes(j)], buf.at[j, me], send2.at[index], recv2.at[index], sib)
        copy.start()
        second.append(copy)

    gain_row = gain_ref[...]
    gain_col = jnp.broadcast_to(gain_row, (128, 128)).T
    basis_t = start_ref[...].T

    acc = jnp.zeros((256, 256), F32)
    for copy in local:
        copy.wait()
    mine = buf.at[me].reshape(128 * rows, 128)
    for a in range(2):
        for rel in range(3):
            first[rel, a].wait_recv()
        for pair in range(layers // 2):
            block = []
            for l in (2 * pair, 2 * pair + 1):
                x = mine[pl.ds(a * layers + l, 128, stride=rows), :]
                hi, lo = split_two(x)
                y = jnp.concatenate([hi, lo], axis=0)
                parts[me, a * layers + l] = y
                block.append(y)
            both = jnp.concatenate(block, axis=1)
            acc = acc + lax.dot_general(both, both, (((1,), (1,)), ((), ())),
                                        preferred_element_type=F32)
    gram_part[...] = (acc[:128, :128] + acc[128:, 128:]) + (acc[:128, 128:] + acc[128:, :128])

    def own_rows(g):
        return pl.ds(pl.multiple_of(g * own, own), own)

    scatter = []
    for rel in (1, 2, 0):
        copy = remote(gram_part.at[own_rows(others[rel])], scattered.at[rel], rs_send.at[rel],
                      rs_recv.at[rel], others[rel])
        copy.start()
        scatter.append(copy)
    relay_a = remote(buf.at[me, pl.ds(base, 2)], buf.at[me, pl.ds(base, 2)], relay_send.at[0],
                     relay_recv.at[0], sib)
    relay_a.start()
    for copy in scatter:
        copy.wait_recv()
    slots[my_cell] = (gram_part[own_rows(me), :] + scattered[0]) + (scattered[1] + scattered[2])

    def broadcast(step):
        other = lax.rem(my_cell + step, cells)
        return pltpu.make_async_remote_copy(
            src_ref=slots.at[my_cell], dst_ref=slots.at[my_cell], send_sem=bc_send.at[other],
            recv_sem=bc_recv.at[my_cell], device_id={"cells": other}, device_id_type=MESH)

    def arrival(step):
        other = lax.rem(my_cell + step, cells)
        return pltpu.make_async_remote_copy(
            src_ref=slots.at[other], dst_ref=slots.at[other], send_sem=bc_send.at[other],
            recv_sem=bc_recv.at[other], device_id={"cells": other}, device_id_type=MESH)

    def start_broadcast(step, carry):
        broadcast(step).start()
        return carry

    def wait_broadcast(step, carry):
        arrival(step).wait_recv()
        return carry

    def wait_sent(step, carry):
        broadcast(step).wait_send()
        return carry

    lax.fori_loop(1, cells, start_broadcast, 0)

    across = []
    for rel, j in ((1, me), (2, sib)):
        copy = remote(field.at[:, :, :, lanes(j)], buf.at[j, me], send2.at[2 + rel], recv2.at[2 + rel],
                      others[rel])
        copy.start()
        across.append(copy)

    def prepare(j, g):
        source = buf.at[j, g].reshape(own * rows, 128)
        for r in range(rows):
            hi, lo = split_two(source[pl.ds(r, own, stride=rows), :])
            parts[j, r, own_rows(g), :] = hi
            parts[j, r, pl.ds(pl.multiple_of(128 + g * own, own), own), :] = lo

    for j in (sib, peer, cross):
        prepare(j, me)
    for copy in second:
        copy.wait_recv()
    for j in (sib, peer, cross):
        prepare(j, sib)

    lax.fori_loop(1, cells, wait_broadcast, 0)

    def add(step, total):
        return total + slots[step]

    gram_full[own_rows(me), :] = lax.fori_loop(1, cells, add, slots[0])
    gather = []
    for rel in (1, 2, 0):
        copy = remote(gram_full.at[own_rows(me)], gram_full.at[own_rows(me)], ag_send.at[rel],
                      ag_recv.at[rel], others[rel])
        copy.start()
        gather.append(copy)
    for copy in gather:
        copy.wait_recv()

    gram = gram_full[...] * gain_row * gain_col * (1.0 / total_rows)
    basis_t = lax.fori_loop(0, ITERS - 1, lambda step, b: refine_step(gram, b), basis_t)

    for copy in across:
        copy.wait_recv()
    relay_b = remote(buf.at[peer, pl.ds(base, 2)], buf.at[peer, pl.ds(base, 2)], relay_send.at[1],
                     relay_recv.at[1], sib)
    relay_b.start()
    basis_t = refine_step(gram, basis_t)
    proj_ref[...] = lax.dot_general(basis_t, basis_t, (((0,), (0,)), ((), ())), precision=HIGH,
                                    preferred_element_type=F32)
    hi, lo = split_two(proj_ref[own_rows(me), :] * gain_row)
    weights = jnp.concatenate([jnp.concatenate([hi, hi], axis=1),
                               jnp.concatenate([lo, jnp.zeros_like(lo)], axis=1)], axis=0)

    relay_a.wait_recv()
    for g in (peer, cross):
        prepare(peer, g)
        prepare(sib, g)
    relay_b.wait_recv()
    for g in (peer, cross):
        prepare(cross, g)

    written = []
    for index, j in enumerate((me,) + others):
        target = out_buf.at[j].reshape(own * rows, 128)
        for r in range(0, rows, 2):
            both = jnp.concatenate([parts[j, r], parts[j, r + 1]], axis=1)
            result = jnp.dot(weights, both, preferred_element_type=F32)
            result = result[:own] + result[own:]
            target[pl.ds(r, own, stride=rows), :] = result[:, :128]
            target[pl.ds(r + 1, own, stride=rows), :] = result[:, 128:]
        copy = pltpu.make_async_copy(out_buf.at[j], out.at[:, :, :, lanes(j)], out_sem.at[index])
        copy.start()
        written.append(copy)

    for copy in list(first.values()) + second + across + scatter + gather + [relay_a, relay_b]:
        copy.wait_send()
    lax.fori_loop(1, cells, wait_sent, 0)
    for copy in written:
        copy.wait()


def per_device(field, period_gain, start_basis):
    cells = lax.axis_size("cells")
    own, _, layers, width = field.shape
    total_rows = 2.0 * layers * width * cells
    any_space = pl.BlockSpec(memory_space=pl.ANY)
    vmem = pl.BlockSpec(memory_space=pltpu.VMEM)
    dma = pltpu.SemaphoreType.DMA
    return pl.pallas_call(
        functools.partial(kernel, cells, total_rows),
        out_shape=jax.ShapeDtypeStruct(field.shape, F32),
        in_specs=[any_space, vmem, vmem],
        out_specs=any_space,
        scratch_shapes=[
            pltpu.VMEM((4, 4, own, 2, layers, 128), F32),
            pltpu.VMEM((4, 2 * layers, 256, 128), BF16),
            pltpu.VMEM((4, own, 2, layers, 128), F32),
            pltpu.VMEM((128, 128), F32),
            pltpu.VMEM((3, own, 128), F32),
            pltpu.VMEM((cells, own, 128), F32),
            pltpu.VMEM((128, 128), F32),
            pltpu.VMEM((128, 128), F32),
            dma((4,)), dma((4,)),
            dma((3, 2)), dma((3, 2)),
            dma((5,)), dma((5,)),
            dma((2,)), dma((2,)),
            dma((3,)), dma((3,)),
            dma((cells,)), dma((cells,)),
            dma((3,)), dma((3,)),
        ],
        compiler_params=pltpu.CompilerParams(
            collective_id=0, has_side_effects=True, vmem_limit_bytes=40 * 1024 * 1024),
        name="factor_and_project",
    )(field, period_gain.reshape(1, -1), start_basis)


def solution(mesh):
    in_specs = (P("per", None, None, "cells"), P(), P())
    out_specs = P("per", None, None, "cells")
    return jax.shard_map(
        per_device, mesh=mesh, in_specs=in_specs, out_specs=out_specs, check_vma=False
    )
```

time: 202 us -> 51.1 us (0.25)
  waiting for transfers between devices: 118 us -> 0 us
  Pallas kernels: 0 us -> 47.8 us
  blocking collectives: 36.7 us -> 0 us
  other arithmetic: 21.9 us -> 0 us
  between operations: 13.6 us -> 0.03 us
  matrix products: 5.55 us -> 0 us
  local copies, waits for them, and re-layouts: 6.11 us -> 3.02 us
    psum x1 -> x0, waiting for transfers between devices: 118 us -> none  [per_device(): gram = lax.psum(local_gram, ('cells', 'per'))]
    pallas_call x0 -> x1, Pallas kernels: none -> 47.8 us  [per_device(): pl.pallas_call(functools.partial(kernel, cells, total_rows), out_shape=ja...]
    all_to_all x2 -> x0, blocking collectives: 36.7 us -> none  [the longest x1 18.5 us: per_device(): lax.all_to_all(scaled, 'per', split_axis=2, concat_axis=0, tiled=True)]
    another operation x15 -> x0, other arithmetic: 20.1 us -> none  [the longest x9 10.8 us: refine(): lower = jnp.linalg.cholesky(inner)]
    dot_general x9 -> x0, matrix products: 4.85 us -> none  [the longest x1 1.61 us: per_device(): lax.dot_general(flat, flat, (((1,), (1,)), ((), ())), precision=HIGH)]
    all_to_all x3 -> x0, local copies, waits for them, and re-layouts: 3.11 us -> none  [the longest x2 2.3 us: per_device(): lax.all_to_all(result, 'per', split_axis=0, concat_axis=2, tiled=True)]
    unnamed x6, local copies, waits for them, and re-layouts: 0.67 us -> 3.02 us
  transfers between devices with their start and end apart: 1 -> 0, of which waited for: 1 -> 0; matrix products, arithmetic and copies ran while one was open for 0% -> 0% of each run, Pallas kernels for 0% -> 0%
where the time goes in v1:
time: 51.1 us; the launch traced here: 50.8 us
  Pallas kernels  47.8 us (94%)
  local copies, waits for them, and re-layouts  3.02 us (6%)
    pallas_call x1, Pallas kernels, per_device(): pl.pallas_call(functools.partial(kernel, cells, total_rows), out_shape=ja...  47.8 us
    unnamed x6, local copies, waits for them, and re-layouts  3.02 us

profile of v1, /device:TPU:0, one launch (start us, length us, event | category | flops | bytes accessed | tf_op | source)
XLA Modules:
  0.0 50.8 jit_solution(496301691406594398)
XLA Ops:
  0.0 0.0 copy-start.1
  0.0 0.8 %copy.4.start_ref = f32[128,32]{1,0:T(8,128)S(1)} copy(f32[128,32]{0,1:T(8,128)} %param.5) | data formatting | bytes 32768 | tf_op args[2]
  0.8 0.0 copy-done.1
  0.8 0.0 copy-start
  0.8 1.2 %copy-done = f32[32,2,8,512]{3,2,1,0:T(8,128)S(1)} copy-done((f32[32,2,8,512]{3,2,1,0:T(8,128)S(1)}, f32[32,2,8,512]{3,2,1,0:T(8,128)}, u32[]{:S(2)}) %copy-start) | copy-done | bytes 1048600
  2.1 47.8 %factor_and_project.1 = f32[32,2,8,512]{3,2,1,0:T(8,128)S(1)} custom-call(f32[32,2,8,512]{3,2,1,0:T(8,128)S(1)} %copy-done, f32[1,128]{1,0:T(1,128)S(1)} %bitcast.1, f32[128,32]{1,0:T(8,128)S(1)} %copy.4.start_ref), custom_call_target="tpu_custom_call" | custom-call | tf_op jit(solution)/shard_map/factor_and_project/pallas_call | solution.py:246
  49.9 1.0 %copy.6 = f32[32,2,8,512]{3,2,1,0:T(8,128)} copy(f32[32,2,8,512]{3,2,1,0:T(8,128)S(1)} %factor_and_project.1) | data formatting | bytes 2097152
Async XLA Ops:
  0.0 0.8 %copy-start.1 = (f32[128]{0:T(128)S(1)}, f32[128]{0:T(128)}, u32[]{:S(2)}) copy-start(f32[128]{0:T(128)} %param.4) | copy-start | bytes 1540
  0.8 1.2 %copy-start = (f32[32,2,8,512]{3,2,1,0:T(8,128)S(1)}, f32[32,2,8,512]{3,2,1,0:T(8,128)}, u32[]{:S(2)}) copy-start(f32[32,2,8,512]{3,2,1,0:T(8,128)} %field.1) | copy-start | bytes 3145732

commit v2 on v1

--- a/solution.py
+++ b/solution.py
@@ -18,27 +18,87 @@
     return hi, (x - hi.astype(F32)).astype(BF16)
 
 
-def refine_step(gram, basis_t):
+def split_three(x):
+    first = x.astype(BF16)
+    rest = x - first.astype(F32)
+    second = rest.astype(BF16)
+    return first, second, (rest - second.astype(F32)).astype(BF16)
+
+
+def beside(*blocks):
+    return jnp.concatenate(blocks, axis=1)
+
+
+def above(*blocks):
+    return jnp.concatenate(blocks, axis=0)
+
+
+def gram_weights(gram):
+    first, second, third = split_three(gram)
+    return above(beside(first, third), beside(second, jnp.zeros_like(second)))
+
+
+def inverse_of(x):
+    guess = pl.reciprocal(x, approx=True)
+    return guess * (2.0 - x * guess)
+
+
+def eliminate(grown, inner):
+    tiles = grown.shape[0] // 8
+    width = grown.shape[1]
+    x = [grown[8 * t:8 * t + 8] for t in range(tiles)]
+    a = [inner[8 * t:8 * t + 8] for t in range(tiles)]
+    row_id = lax.broadcasted_iota(jnp.int32, (8, width), 0)
+    for t in range(tiles):
+        column = {}
+        for j in range(8):
+            for s in range(t, tiles):
+                column[j, s] = jnp.broadcast_to(a[s][:, 8 * t + j:8 * t + j + 1], (8, width))
+        pivots = jnp.ones((8, width), F32)
+        for j in range(8):
+            inverse = inverse_of(jnp.broadcast_to(column[j, t][j:j + 1], (8, width)))
+            pivots = jnp.where(row_id == j, column[j, t], pivots)
+            factor = {s: column[j, s] * inverse for s in range(t, tiles)}
+            factor[t] = jnp.where(row_id > j, factor[t], 0.0)
+            later = {i: jnp.broadcast_to(column[i, t][j:j + 1], (8, width)) for i in range(j + 1, 8)}
+            x_row = jnp.broadcast_to(x[t][j:j + 1], (8, width))
+            a_row = jnp.broadcast_to(a[t][j:j + 1], a[t].shape)
+            for s in range(t, tiles):
+                for i in range(j + 1, 8):
+                    column[i, s] = column[i, s] - factor[s] * later[i]
+                x[s] = x[s] - factor[s] * x_row
+                if s > t:
+                    a[s] = a[s] - factor[s][:, :a_row.shape[1]] * a_row
+            if t < tiles - 1:
+                a[t] = a[t] - factor[t][:, :a_row.shape[1]] * a_row
+        x[t] = x[t] * lax.rsqrt(pivots)
+    return above(*x)
+
+
+def refine_step(weights, basis_t):
     rank, periods = basis_t.shape
-    grown = jnp.dot(basis_t, gram, precision=HIGH, preferred_element_type=F32)
-    inner = lax.dot_general(grown, grown, (((1,), (1,)), ((), ())), precision=HIGH,
-                            preferred_element_type=F32)
-    row_id = lax.broadcasted_iota(jnp.int32, (rank, 1), 0)
-    for k in range(rank - 1):
-        below = jnp.where(row_id > k, inner[:, k:k + 1], 0.0)
-        inverse = 1.0 / inner[k:k + 1, k:k + 1]
-        grown_row = grown[k:k + 1, :] * inverse
-        inner_row = inner[k:k + 1, :] * inverse
-        grown = grown - below * grown_row
-        inner = inner - below * inner_row
-    eye = lax.broadcasted_iota(jnp.int32, (rank, rank), 0) == lax.broadcasted_iota(
-        jnp.int32, (rank, rank), 1)
-    pivots = jnp.sum(jnp.where(eye, inner, 0.0), axis=1, keepdims=True)
-    return grown * lax.rsqrt(pivots)
-
-
-def kernel(cells, total_rows, field, gain_ref, start_ref, out, buf, parts, out_buf, gram_part,
-           scattered, slots, gram_full, proj_ref, local_sem, out_sem, send1, recv1, send2, recv2,
+    b1, b2, b3 = split_three(basis_t)
+    zero = jnp.zeros_like(b1)
+    product = jnp.dot(above(beside(b1, b1), beside(b2, b2), beside(b3, zero)), weights,
+                      preferred_element_type=F32)
+    low, high = product[:, :periods], product[:, periods:]
+    grown = low[:rank] + ((low[rank:2 * rank] + high[:rank]) + (low[2 * rank:] + high[rank:2 * rank]))
+    g1, g2, g3 = split_three(grown)
+    product = lax.dot_general(
+        above(beside(g1, g1, g1), beside(g2, g2, zero), beside(g3, zero, zero)),
+        beside(g1, g2, g3), (((1,), (1,)), ((), ())), preferred_element_type=F32)
+    inner = product[:rank] + (product[rank:2 * rank] + product[2 * rank:])
+    return eliminate(grown, inner)
+
+
+def outer_of(basis_t):
+    q1, q2, q3 = split_three(basis_t)
+    return lax.dot_general(above(q1, q1, q1, q2, q2, q3), above(q1, q2, q3, q1, q2, q1),
+                           (((0,), (0,)), ((), ())), preferred_element_type=F32)
+
+
+def kernel(cells, total_rows, field, gain_any, start_any, out, buf, parts, out_buf, gain_ref, start_ref, gram_part,
+           scattered, slots, gram_full, proj_ref, local_sem, small_sem, out_sem, send1, recv1, send2, recv2,
            relay_send, relay_recv, rs_send, rs_recv, bc_send, bc_recv, ag_send, ag_recv):
     me = lax.axis_index("per")
     my_cell = lax.axis_index("cells")
@@ -60,6 +120,11 @@
         copy.start()
         local.append(copy)
 
+    small = [pltpu.make_async_copy(gain_any, gain_ref, small_sem.at[0]),
+             pltpu.make_async_copy(start_any, start_ref, small_sem.at[1])]
+    for copy in small:
+        copy.start()
+
     barrier = pltpu.get_barrier_semaphore()
     for other in others:
         pl.semaphore_signal(barrier, inc=1, device_id={"per": other}, device_id_type=MESH)
@@ -91,9 +156,11 @@
         copy.start()
         second.append(copy)
 
+    for copy in small:
+        copy.wait()
     gain_row = gain_ref[...]
     gain_col = jnp.broadcast_to(gain_row, (128, 128)).T
-    basis_t = start_ref[...].T
+    basis_t = start_ref[...]
 
     acc = jnp.zeros((256, 256), F32)
     for copy in local:
@@ -193,39 +260,38 @@
     for copy in gather:
         copy.wait_recv()
 
-    gram = gram_full[...] * gain_row * gain_col * (1.0 / total_rows)
-    basis_t = lax.fori_loop(0, ITERS - 1, lambda step, b: refine_step(gram, b), basis_t)
-
+    weights = gram_weights(gram_full[...] * gain_row * gain_col * (1.0 / total_rows))
+    basis_t = refine_step(weights, basis_t)
+    relay_a.wait_recv()
+    for g in (peer, cross):
+        prepare(sib, g)
+    for step in range(1, ITERS - 1):
+        basis_t = refine_step(weights, basis_t)
     for copy in across:
         copy.wait_recv()
     relay_b = remote(buf.at[peer, pl.ds(base, 2)], buf.at[peer, pl.ds(base, 2)], relay_send.at[1],
                      relay_recv.at[1], sib)
     relay_b.start()
-    basis_t = refine_step(gram, basis_t)
-    proj_ref[...] = lax.dot_general(basis_t, basis_t, (((0,), (0,)), ((), ())), precision=HIGH,
-                                    preferred_element_type=F32)
-    hi, lo = split_two(proj_ref[own_rows(me), :] * gain_row)
-    weights = jnp.concatenate([jnp.concatenate([hi, hi], axis=1),
-                               jnp.concatenate([lo, jnp.zeros_like(lo)], axis=1)], axis=0)
-
-    relay_a.wait_recv()
     for g in (peer, cross):
         prepare(peer, g)
-        prepare(sib, g)
-    relay_b.wait_recv()
-    for g in (peer, cross):
-        prepare(cross, g)
+    basis_t = refine_step(weights, basis_t)
+    proj_ref[...] = outer_of(basis_t)
+    hi, lo = split_two(proj_ref[own_rows(me), :] * gain_row)
+    weights = above(beside(hi, hi), beside(lo, jnp.zeros_like(lo)))
 
     written = []
     for index, j in enumerate((me,) + others):
+        if index == 3:
+            relay_b.wait_recv()
+            for g in (peer, cross):
+                prepare(cross, g)
         target = out_buf.at[j].reshape(own * rows, 128)
         for r in range(0, rows, 2):
-            both = jnp.concatenate([parts[j, r], parts[j, r + 1]], axis=1)
-            result = jnp.dot(weights, both, preferred_element_type=F32)
+            result = jnp.dot(weights, beside(parts[j, r], parts[j, r + 1]), preferred_element_type=F32)
             result = result[:own] + result[own:]
             target[pl.ds(r, own, stride=rows), :] = result[:, :128]
             target[pl.ds(r + 1, own, stride=rows), :] = result[:, 128:]
-        copy = pltpu.make_async_copy(out_buf.at[j], out.at[:, :, :, lanes(j)], out_sem.at[index])
+        copy = pltpu.make_async_copy(out_buf.at[j], out.at[j], out_sem.at[index])
         copy.start()
         written.append(copy)
 
@@ -241,23 +307,24 @@
     own, _, layers, width = field.shape
     total_rows = 2.0 * layers * width * cells
     any_space = pl.BlockSpec(memory_space=pl.ANY)
-    vmem = pl.BlockSpec(memory_space=pltpu.VMEM)
     dma = pltpu.SemaphoreType.DMA
-    return pl.pallas_call(
+    result = pl.pallas_call(
         functools.partial(kernel, cells, total_rows),
-        out_shape=jax.ShapeDtypeStruct(field.shape, F32),
-        in_specs=[any_space, vmem, vmem],
+        out_shape=jax.ShapeDtypeStruct((4, own, 2, layers, 128), F32),
+        in_specs=[any_space, any_space, any_space],
         out_specs=any_space,
         scratch_shapes=[
             pltpu.VMEM((4, 4, own, 2, layers, 128), F32),
             pltpu.VMEM((4, 2 * layers, 256, 128), BF16),
             pltpu.VMEM((4, own, 2, layers, 128), F32),
+            pltpu.VMEM((1, 128), F32),
+            pltpu.VMEM(start_basis.shape[::-1], F32),
             pltpu.VMEM((128, 128), F32),
             pltpu.VMEM((3, own, 128), F32),
             pltpu.VMEM((cells, own, 128), F32),
             pltpu.VMEM((128, 128), F32),
             pltpu.VMEM((128, 128), F32),
-            dma((4,)), dma((4,)),
+            dma((4,)), dma((2,)), dma((4,)),
             dma((3, 2)), dma((3, 2)),
             dma((5,)), dma((5,)),
             dma((2,)), dma((2,)),
@@ -266,9 +333,10 @@
             dma((3,)), dma((3,)),
         ],
         compiler_params=pltpu.CompilerParams(
-            collective_id=0, has_side_effects=True, vmem_limit_bytes=40 * 1024 * 1024),
+            collective_id=0, has_side_effects=True, vmem_limit_bytes=56 * 1024 * 1024),
         name="factor_and_project",
-    )(field, period_gain.reshape(1, -1), start_basis)
+    )(field, period_gain.reshape(1, -1), start_basis.T)
+    return result.transpose(1, 2, 3, 0, 4).reshape(field.shape)
 
 
 def solution(mesh):

time: 51.1 us -> 45 us (0.88)
  Pallas kernels: 47.8 us -> 42.5 us
  local copies, waits for them, and re-layouts: 3.02 us -> 2.34 us
    pallas_call x1, Pallas kernels: 47.8 us -> 42.5 us  [per_device(): pl.pallas_call(functools.partial(kernel, cells, total_rows), out_shape=ja...]
    unnamed x6 -> x0, local copies, waits for them, and re-layouts: 3.02 us -> none
    reshape x0 -> x1, local copies, waits for them, and re-layouts: none -> 2.34 us  [per_device(): return result.transpose(1, 2, 3, 0, 4).reshape(field.shape)]
where the time goes in v2:
time: 45 us; the launch traced here: 44.9 us
  Pallas kernels  42.5 us (94%)
  local copies, waits for them, and re-layouts  2.34 us (5%)
    pallas_call x1, Pallas kernels, per_device(): pl.pallas_call(functools.partial(kernel, cells, total_rows), out_shape=ja...  42.5 us
    reshape x1, local copies, waits for them, and re-layouts, per_device(): return result.transpose(1, 2, 3, 0, 4).reshape(field.shape)  2.34 us

profile of v2, /device:TPU:0, one launch (start us, length us, event | category | flops | bytes accessed | tf_op | source)
XLA Modules:
  0.0 44.9 jit_solution(8901141437409762415)
XLA Ops:
  0.0 42.5 %factor_and_project.1 = f32[4,32,2,8,128]{4,3,2,1,0:T(8,128)} custom-call(f32[32,2,8,512]{3,2,1,0:T(8,128)} %field.1, f32[1,128]{1,0:T(1,128)} %bitcast.8, f32[32,128]{1,0:T(8,128)} %bitcast.7), custom_call_target="tpu_custom_call" | custom-call | tf_op jit(solution)/shard_map/factor_and_project/pallas_call | solution.py:311
  42.5 2.3 %copy_bitcast_fusion = f32[32,2,8,512]{3,2,1,0:T(8,128)} fusion(f32[4,32,2,8,128]{4,3,2,1,0:T(8,128)} %factor_and_project.1), kind=kLoop, calls=%fused_computation | loop fusion | bytes 2097152 | tf_op jit(solution)/shard_map/reshape | solution.py:339

commit v3 on v2

--- a/solution.py
+++ b/solution.py
@@ -98,7 +98,7 @@
 
 
 def kernel(cells, total_rows, field, gain_any, start_any, out, buf, parts, out_buf, gain_ref, start_ref, gram_part,
-           scattered, slots, gram_full, proj_ref, local_sem, small_sem, out_sem, send1, recv1, send2, recv2,
+           scattered, slots, gram_full, proj_ref, local_sem, small_sem, out_sem, send1, recv1, send2, recv2, send3, recv3,
            relay_send, relay_recv, rs_send, rs_recv, bc_send, bc_recv, ag_send, ag_recv):
     me = lax.axis_index("per")
     my_cell = lax.axis_index("cells")
@@ -126,16 +126,24 @@
         copy.start()
 
     barrier = pltpu.get_barrier_semaphore()
-    for other in others:
-        pl.semaphore_signal(barrier, inc=1, device_id={"per": other}, device_id_type=MESH)
+    parity = lax.rem(my_cell, 2)
+    half = my_cell // 2
+    halves = cells // 2
+    pair_cell = my_cell + 1 - 2 * parity
+    group = [(g, c) for c in (my_cell, pair_cell) for g in (me,) + others]
+    for g, c in group[1:]:
+        pl.semaphore_signal(barrier, inc=1, device_id={"per": g, "cells": c}, device_id_type=MESH)
+
+    def distant(step):
+        return lax.rem(half + step, halves)
 
     def greet(step, carry):
-        pl.semaphore_signal(barrier, inc=1, device_id={"cells": lax.rem(my_cell + step, cells)},
+        pl.semaphore_signal(barrier, inc=1, device_id={"cells": 2 * distant(step) + parity},
                             device_id_type=MESH)
         return carry
 
-    lax.fori_loop(1, cells, greet, 0)
-    pl.semaphore_wait(barrier, 3 + cells - 1)
+    lax.fori_loop(1, halves, greet, 0)
+    pl.semaphore_wait(barrier, 7 + halves - 1)
 
     def remote(src, dst, send, recv, other):
         return pltpu.make_async_remote_copy(src_ref=src, dst_ref=dst, send_sem=send, recv_sem=recv,
@@ -185,10 +193,21 @@
     def own_rows(g):
         return pl.ds(pl.multiple_of(g * own, own), own)
 
+    def share(g, c):
+        return pl.ds(pl.multiple_of((lax.rem(c, 2) * 4 + g) * (own // 2), own // 2), own // 2)
+
+    def to_group(src, dst, send, recv, g, c):
+        return pltpu.make_async_remote_copy(src_ref=src, dst_ref=dst, send_sem=send, recv_sem=recv,
+                                            device_id={"per": g, "cells": c}, device_id_type=MESH)
+
+    order = (6, 7, 5, 4, 2, 3, 1)
+    mine_only = share(me, my_cell)
+
     scatter = []
-    for rel in (1, 2, 0):
-        copy = remote(gram_part.at[own_rows(others[rel])], scattered.at[rel], rs_send.at[rel],
-                      rs_recv.at[rel], others[rel])
+    for rel in order:
+        g, c = group[rel]
+        copy = to_group(gram_part.at[share(g, c)], scattered.at[rel], rs_send.at[rel],
+                        rs_recv.at[rel], g, c)
         copy.start()
         scatter.append(copy)
     relay_a = remote(buf.at[me, pl.ds(base, 2)], buf.at[me, pl.ds(base, 2)], relay_send.at[0],
@@ -196,19 +215,20 @@
     relay_a.start()
     for copy in scatter:
         copy.wait_recv()
-    slots[my_cell] = (gram_part[own_rows(me), :] + scattered[0]) + (scattered[1] + scattered[2])
+    slots[half] = ((gram_part[mine_only, :] + scattered[1]) + (scattered[2] + scattered[3])) + (
+        (scattered[4] + scattered[5]) + (scattered[6] + scattered[7]))
 
     def broadcast(step):
-        other = lax.rem(my_cell + step, cells)
+        other = distant(step)
         return pltpu.make_async_remote_copy(
-            src_ref=slots.at[my_cell], dst_ref=slots.at[my_cell], send_sem=bc_send.at[other],
-            recv_sem=bc_recv.at[my_cell], device_id={"cells": other}, device_id_type=MESH)
+            src_ref=slots.at[half], dst_ref=slots.at[half], send_sem=bc_send.at[other],
+            recv_sem=bc_recv.at[half], device_id={"cells": 2 * other + parity}, device_id_type=MESH)
 
     def arrival(step):
-        other = lax.rem(my_cell + step, cells)
+        other = distant(step)
         return pltpu.make_async_remote_copy(
             src_ref=slots.at[other], dst_ref=slots.at[other], send_sem=bc_send.at[other],
-            recv_sem=bc_recv.at[other], device_id={"cells": other}, device_id_type=MESH)
+            recv_sem=bc_recv.at[other], device_id={"cells": 2 * other + parity}, device_id_type=MESH)
 
     def start_broadcast(step, carry):
         broadcast(step).start()
@@ -222,14 +242,27 @@
         broadcast(step).wait_send()
         return carry
 
-    lax.fori_loop(1, cells, start_broadcast, 0)
-
-    across = []
-    for rel, j in ((1, me), (2, sib)):
-        copy = remote(field.at[:, :, :, lanes(j)], buf.at[j, me], send2.at[2 + rel], recv2.at[2 + rel],
-                      others[rel])
-        copy.start()
-        across.append(copy)
+    lax.fori_loop(1, halves, start_broadcast, 0)
+
+    across = {}
+    for a in range(2):
+        for rel, j in ((1, me), (2, sib)):
+            across[rel, a] = remote(field.at[:, a, :, lanes(j)], buf.at[j, me, :, a],
+                                    send3.at[rel - 1, a], recv3.at[rel - 1, a], others[rel])
+
+    def start_across(a):
+        for rel in (1, 2):
+            across[rel, a].start()
+
+    def relay_across(a):
+        for rel in (1, 2):
+            across[rel, a].wait_recv()
+        place = buf.at[peer, pl.ds(base, 2), :, a]
+        copy = remote(place, place, relay_send.at[1 + a], relay_recv.at[1 + a], sib)
+        copy.start()
+        return copy
+
+    start_across(0)
 
     def prepare(j, g):
         source = buf.at[j, g].reshape(own * rows, 128)
@@ -245,44 +278,43 @@
     for j in (sib, peer, cross):
         prepare(j, sib)
 
-    lax.fori_loop(1, cells, wait_broadcast, 0)
+    lax.fori_loop(1, halves, wait_broadcast, 0)
 
     def add(step, total):
         return total + slots[step]
 
-    gram_full[own_rows(me), :] = lax.fori_loop(1, cells, add, slots[0])
+    gram_full[mine_only, :] = lax.fori_loop(1, halves, add, slots[0])
     gather = []
-    for rel in (1, 2, 0):
-        copy = remote(gram_full.at[own_rows(me)], gram_full.at[own_rows(me)], ag_send.at[rel],
-                      ag_recv.at[rel], others[rel])
+    for rel in order:
+        g, c = group[rel]
+        copy = to_group(gram_full.at[mine_only], gram_full.at[mine_only], ag_send.at[rel],
+                        ag_recv.at[rel], g, c)
         copy.start()
         gather.append(copy)
     for copy in gather:
         copy.wait_recv()
 
+    start_across(1)
     weights = gram_weights(gram_full[...] * gain_row * gain_col * (1.0 / total_rows))
     basis_t = refine_step(weights, basis_t)
     relay_a.wait_recv()
     for g in (peer, cross):
         prepare(sib, g)
-    for step in range(1, ITERS - 1):
+    relays = [relay_across(0)]
+    for step in range(1, ITERS):
         basis_t = refine_step(weights, basis_t)
-    for copy in across:
-        copy.wait_recv()
-    relay_b = remote(buf.at[peer, pl.ds(base, 2)], buf.at[peer, pl.ds(base, 2)], relay_send.at[1],
-                     relay_recv.at[1], sib)
-    relay_b.start()
-    for g in (peer, cross):
-        prepare(peer, g)
-    basis_t = refine_step(weights, basis_t)
+    relays.append(relay_across(1))
     proj_ref[...] = outer_of(basis_t)
     hi, lo = split_two(proj_ref[own_rows(me), :] * gain_row)
     weights = above(beside(hi, hi), beside(lo, jnp.zeros_like(lo)))
 
+    for g in (peer, cross):
+        prepare(peer, g)
     written = []
     for index, j in enumerate((me,) + others):
         if index == 3:
-            relay_b.wait_recv()
+            for copy in relays:
+                copy.wait_recv()
             for g in (peer, cross):
                 prepare(cross, g)
         target = out_buf.at[j].reshape(own * rows, 128)
@@ -291,13 +323,13 @@
             result = result[:own] + result[own:]
             target[pl.ds(r, own, stride=rows), :] = result[:, :128]
             target[pl.ds(r + 1, own, stride=rows), :] = result[:, 128:]
-        copy = pltpu.make_async_copy(out_buf.at[j], out.at[j], out_sem.at[index])
+        copy = pltpu.make_async_copy(out_buf.at[j], out.at[:, :, :, lanes(j)], out_sem.at[index])
         copy.start()
         written.append(copy)
 
-    for copy in list(first.values()) + second + across + scatter + gather + [relay_a, relay_b]:
+    for copy in list(first.values()) + second + list(across.values()) + scatter + gather + [relay_a] + relays:
         copy.wait_send()
-    lax.fori_loop(1, cells, wait_sent, 0)
+    lax.fori_loop(1, halves, wait_sent, 0)
     for copy in written:
         copy.wait()
 
@@ -308,9 +340,9 @@
     total_rows = 2.0 * layers * width * cells
     any_space = pl.BlockSpec(memory_space=pl.ANY)
     dma = pltpu.SemaphoreType.DMA
-    result = pl.pallas_call(
+    return pl.pallas_call(
         functools.partial(kernel, cells, total_rows),
-        out_shape=jax.ShapeDtypeStruct((4, own, 2, layers, 128), F32),
+        out_shape=jax.ShapeDtypeStruct(field.shape, F32),
         in_specs=[any_space, any_space, any_space],
         out_specs=any_space,
         scratch_shapes=[
@@ -320,23 +352,23 @@
             pltpu.VMEM((1, 128), F32),
             pltpu.VMEM(start_basis.shape[::-1], F32),
             pltpu.VMEM((128, 128), F32),
-            pltpu.VMEM((3, own, 128), F32),
-            pltpu.VMEM((cells, own, 128), F32),
+            pltpu.VMEM((8, own // 2, 128), F32),
+            pltpu.VMEM((cells // 2, own // 2, 128), F32),
             pltpu.VMEM((128, 128), F32),
             pltpu.VMEM((128, 128), F32),
             dma((4,)), dma((2,)), dma((4,)),
             dma((3, 2)), dma((3, 2)),
-            dma((5,)), dma((5,)),
-            dma((2,)), dma((2,)),
             dma((3,)), dma((3,)),
-            dma((cells,)), dma((cells,)),
+            dma((2, 2)), dma((2, 2)),
             dma((3,)), dma((3,)),
+            dma((8,)), dma((8,)),
+            dma((cells // 2,)), dma((cells // 2,)),
+            dma((8,)), dma((8,)),
         ],
         compiler_params=pltpu.CompilerParams(
             collective_id=0, has_side_effects=True, vmem_limit_bytes=56 * 1024 * 1024),
         name="factor_and_project",
     )(field, period_gain.reshape(1, -1), start_basis.T)
-    return result.transpose(1, 2, 3, 0, 4).reshape(field.shape)
 
 
 def solution(mesh):

time: 45 us -> 42.9 us (0.953)
  Pallas kernels: 42.5 us -> 40.4 us
    reshape x1 -> x0, local copies, waits for them, and re-layouts: 2.34 us -> none  [per_device(): return result.transpose(1, 2, 3, 0, 4).reshape(field.shape)]
    unnamed x0 -> x1, local copies, waits for them, and re-layouts: none -> 2.31 us
    pallas_call x1, Pallas kernels: 42.5 us -> 40.4 us  [per_device(): pl.pallas_call(functools.partial(kernel, cells, total_rows), out_shape=ja...]
where the time goes in v3:
time: 42.9 us; the launch traced here: 42.8 us
  Pallas kernels  40.4 us (94%)
  local copies, waits for them, and re-layouts  2.31 us (5%)
    pallas_call x1, Pallas kernels, per_device(): pl.pallas_call(functools.partial(kernel, cells, total_rows), out_shape=ja...  40.4 us
    unnamed x1, local copies, waits for them, and re-layouts  2.31 us

profile of v3, /device:TPU:0, one launch (start us, length us, event | category | flops | bytes accessed | tf_op | source)
XLA Modules:
  0.0 42.8 jit_solution(7686207145908672930)
XLA Ops:
  0.0 40.4 %factor_and_project.1 = f32[32,2,8,512]{3,2,1,0:T(8,128)} custom-call(f32[32,2,8,512]{3,2,1,0:T(8,128)} %field.1, f32[1,128]{1,0:T(1,128)} %bitcast.3, f32[32,128]{1,0:T(8,128)} %bitcast.2), custom_call_target="tpu_custom_call" | custom-call | tf_op jit(solution)/shard_map/factor_and_project/pallas_call | solution.py:343
  40.5 2.3 %copy.5 = f32[32,2,8,512]{3,2,1,0:T(8,128)} copy(f32[32,2,8,512]{3,2,1,0:T(8,128)} %factor_and_project.1) | data formatting | bytes 2097152

commit v4 on v3

--- a/solution.py
+++ b/solution.py
@@ -97,8 +97,8 @@
                            (((0,), (0,)), ((), ())), preferred_element_type=F32)
 
 
-def kernel(cells, total_rows, field, gain_any, start_any, out, buf, parts, out_buf, gain_ref, start_ref, gram_part,
-           scattered, slots, gram_full, proj_ref, local_sem, small_sem, out_sem, send1, recv1, send2, recv2, send3, recv3,
+def kernel(cells, total_rows, field, gain_any, start_any, buf, weights_ref, mine, gain_ref, start_ref, gram_part,
+           scattered, slots, gram_full, proj_ref, local_sem, small_sem, back_sem, send1, recv1, send2, recv2, send3, recv3,
            relay_send, relay_recv, rs_send, rs_recv, bc_send, bc_recv, ag_send, ag_recv):
     me = lax.axis_index("per")
     my_cell = lax.axis_index("cells")
@@ -116,7 +116,8 @@
 
     local = []
     for index, j in enumerate((me,) + others):
-        copy = pltpu.make_async_copy(field.at[:, :, :, lanes(j)], buf.at[j, me], local_sem.at[index])
+        target = mine.at[me] if index == 0 else buf.at[j, me]
+        copy = pltpu.make_async_copy(field.at[:, :, :, lanes(j)], target, local_sem.at[index])
         copy.start()
         local.append(copy)
 
@@ -153,7 +154,7 @@
     for a in range(2):
         for rel in (1, 2, 0):
             other = others[rel]
-            copy = remote(field.at[:, a, :, lanes(other)], buf.at[other, me, :, a],
+            copy = remote(field.at[:, a, :, lanes(other)], mine.at[me, :, a],
                           send1.at[rel, a], recv1.at[rel, a], other)
             copy.start()
             first[rel, a] = copy
@@ -171,21 +172,16 @@
     basis_t = start_ref[...]
 
     acc = jnp.zeros((256, 256), F32)
-    for copy in local:
-        copy.wait()
-    mine = buf.at[me].reshape(128 * rows, 128)
+    local[0].wait()
+    flat = mine.reshape(128 * rows, 128)
     for a in range(2):
         for rel in range(3):
             first[rel, a].wait_recv()
         for pair in range(layers // 2):
             block = []
             for l in (2 * pair, 2 * pair + 1):
-                x = mine[pl.ds(a * layers + l, 128, stride=rows), :]
-                hi, lo = split_two(x)
-                y = jnp.concatenate([hi, lo], axis=0)
-                parts[me, a * layers + l] = y
-                block.append(y)
-            both = jnp.concatenate(block, axis=1)
+                block.append(above(*split_two(flat[pl.ds(a * layers + l, 128, stride=rows), :])))
+            both = beside(*block)
             acc = acc + lax.dot_general(both, both, (((1,), (1,)), ((), ())),
                                         preferred_element_type=F32)
     gram_part[...] = (acc[:128, :128] + acc[128:, 128:]) + (acc[:128, 128:] + acc[128:, :128])
@@ -210,7 +206,9 @@
                         rs_recv.at[rel], g, c)
         copy.start()
         scatter.append(copy)
-    relay_a = remote(buf.at[me, pl.ds(base, 2)], buf.at[me, pl.ds(base, 2)], relay_send.at[0],
+    back = pltpu.make_async_copy(mine, buf.at[me], back_sem.at[0])
+    back.start()
+    relay_a = remote(mine.at[pl.ds(base, 2)], buf.at[me, pl.ds(base, 2)], relay_send.at[0],
                      relay_recv.at[0], sib)
     relay_a.start()
     for copy in scatter:
@@ -244,10 +242,12 @@
 
     lax.fori_loop(1, halves, start_broadcast, 0)
 
+    early = 3 * own // 8
+    pieces = (pl.ds(0, early), pl.ds(early, own - early))
     across = {}
     for a in range(2):
         for rel, j in ((1, me), (2, sib)):
-            across[rel, a] = remote(field.at[:, a, :, lanes(j)], buf.at[j, me, :, a],
+            across[rel, a] = remote(field.at[pieces[a], :, :, lanes(j)], buf.at[j, me, pieces[a]],
                                     send3.at[rel - 1, a], recv3.at[rel - 1, a], others[rel])
 
     def start_across(a):
@@ -257,26 +257,12 @@
     def relay_across(a):
         for rel in (1, 2):
             across[rel, a].wait_recv()
-        place = buf.at[peer, pl.ds(base, 2), :, a]
+        place = buf.at[peer, pl.ds(base, 2), pieces[a]]
         copy = remote(place, place, relay_send.at[1 + a], relay_recv.at[1 + a], sib)
         copy.start()
         return copy
 
     start_across(0)
-
-    def prepare(j, g):
-        source = buf.at[j, g].reshape(own * rows, 128)
-        for r in range(rows):
-            hi, lo = split_two(source[pl.ds(r, own, stride=rows), :])
-            parts[j, r, own_rows(g), :] = hi
-            parts[j, r, pl.ds(pl.multiple_of(128 + g * own, own), own), :] = lo
-
-    for j in (sib, peer, cross):
-        prepare(j, me)
-    for copy in second:
-        copy.wait_recv()
-    for j in (sib, peer, cross):
-        prepare(j, sib)
 
     lax.fori_loop(1, halves, wait_broadcast, 0)
 
@@ -297,41 +283,35 @@
     start_across(1)
     weights = gram_weights(gram_full[...] * gain_row * gain_col * (1.0 / total_rows))
     basis_t = refine_step(weights, basis_t)
-    relay_a.wait_recv()
-    for g in (peer, cross):
-        prepare(sib, g)
     relays = [relay_across(0)]
     for step in range(1, ITERS):
         basis_t = refine_step(weights, basis_t)
     relays.append(relay_across(1))
     proj_ref[...] = outer_of(basis_t)
     hi, lo = split_two(proj_ref[own_rows(me), :] * gain_row)
-    weights = above(beside(hi, hi), beside(lo, jnp.zeros_like(lo)))
-
-    for g in (peer, cross):
-        prepare(peer, g)
-    written = []
-    for index, j in enumerate((me,) + others):
-        if index == 3:
-            for copy in relays:
-                copy.wait_recv()
-            for g in (peer, cross):
-                prepare(cross, g)
-        target = out_buf.at[j].reshape(own * rows, 128)
-        for r in range(0, rows, 2):
-            result = jnp.dot(weights, beside(parts[j, r], parts[j, r + 1]), preferred_element_type=F32)
-            result = result[:own] + result[own:]
-            target[pl.ds(r, own, stride=rows), :] = result[:, :128]
-            target[pl.ds(r + 1, own, stride=rows), :] = result[:, 128:]
-        copy = pltpu.make_async_copy(out_buf.at[j], out.at[:, :, :, lanes(j)], out_sem.at[index])
-        copy.start()
-        written.append(copy)
-
+    weights_ref[...] = above(beside(hi, hi), beside(lo, jnp.zeros_like(lo)))
+
+    for copy in second + [relay_a] + relays:
+        copy.wait_recv()
+    for copy in local[1:] + [back]:
+        copy.wait()
     for copy in list(first.values()) + second + list(across.values()) + scatter + gather + [relay_a] + relays:
         copy.wait_send()
     lax.fori_loop(1, halves, wait_sent, 0)
-    for copy in written:
-        copy.wait()
+
+
+def project(weights_ref, field_ref, out_ref):
+    _, parts, own, _, layers, _ = field_ref.shape
+    rows = 2 * layers
+    source = field_ref.at[0].reshape(parts * own * rows, 128)
+    target = out_ref.reshape(own * rows, 128)
+    weights = weights_ref[...]
+    for r in range(0, rows, 2):
+        block = [above(*split_two(source[pl.ds(r + i, parts * own, stride=rows), :])) for i in range(2)]
+        result = jnp.dot(weights, beside(*block), preferred_element_type=F32)
+        result = result[:own] + result[own:]
+        target[pl.ds(r, own, stride=rows), :] = result[:, :128]
+        target[pl.ds(r + 1, own, stride=rows), :] = result[:, 128:]
 
 
 def per_device(field, period_gain, start_basis):
@@ -340,14 +320,13 @@
     total_rows = 2.0 * layers * width * cells
     any_space = pl.BlockSpec(memory_space=pl.ANY)
     dma = pltpu.SemaphoreType.DMA
-    return pl.pallas_call(
+    gathered, weights = pl.pallas_call(
         functools.partial(kernel, cells, total_rows),
-        out_shape=jax.ShapeDtypeStruct(field.shape, F32),
+        out_shape=(jax.ShapeDtypeStruct((4, 4, own, 2, layers, 128), F32),
+                   jax.ShapeDtypeStruct((2 * own, 256), BF16)),
         in_specs=[any_space, any_space, any_space],
-        out_specs=any_space,
+        out_specs=(any_space, pl.BlockSpec(memory_space=pltpu.VMEM)),
         scratch_shapes=[
-            pltpu.VMEM((4, 4, own, 2, layers, 128), F32),
-            pltpu.VMEM((4, 2 * layers, 256, 128), BF16),
             pltpu.VMEM((4, own, 2, layers, 128), F32),
             pltpu.VMEM((1, 128), F32),
             pltpu.VMEM(start_basis.shape[::-1], F32),
@@ -356,7 +335,7 @@
             pltpu.VMEM((cells // 2, own // 2, 128), F32),
             pltpu.VMEM((128, 128), F32),
             pltpu.VMEM((128, 128), F32),
-            dma((4,)), dma((2,)), dma((4,)),
+            dma((4,)), dma((2,)), dma((1,)),
             dma((3, 2)), dma((3, 2)),
             dma((3,)), dma((3,)),
             dma((2, 2)), dma((2, 2)),
@@ -367,8 +346,18 @@
         ],
         compiler_params=pltpu.CompilerParams(
             collective_id=0, has_side_effects=True, vmem_limit_bytes=56 * 1024 * 1024),
-        name="factor_and_project",
+        name="gather_and_factor",
     )(field, period_gain.reshape(1, -1), start_basis.T)
+    return pl.pallas_call(
+        project,
+        grid=(4,),
+        out_shape=jax.ShapeDtypeStruct(field.shape, F32),
+        in_specs=[pl.BlockSpec((2 * own, 256), lambda j: (0, 0)),
+                  pl.BlockSpec((1, 4, own, 2, layers, 128), lambda j: (j, 0, 0, 0, 0, 0))],
+        out_specs=pl.BlockSpec((own, 2, layers, 128), lambda j: (0, 0, 0, j)),
+        compiler_params=pltpu.CompilerParams(vmem_limit_bytes=56 * 1024 * 1024),
+        name="project",
+    )(weights, gathered)
 
 
 def solution(mesh):

time: 42.9 us -> 46 us (1.072)
  Pallas kernels: 40.4 us -> 45.8 us
  local copies, waits for them, and re-layouts: 2.31 us -> 0 us
    pallas_call x1 -> x2, Pallas kernels: 40.4 us -> 45.8 us  [the longest x1 40.8 us: per_device(): pl.pallas_call(functools.partial(kernel, cells, total_rows), out_shape=(j...]
    unnamed x1 -> x0, local copies, waits for them, and re-layouts: 2.31 us -> none
where the time goes in v4:
time: 46 us; the launch traced here: 45.8 us
  Pallas kernels  45.8 us (100%)
    pallas_call x1, Pallas kernels, per_device(): pl.pallas_call(functools.partial(kernel, cells, total_rows), out_shape=(j...  40.8 us
    pallas_call x1, Pallas kernels, per_device(): pl.pallas_call(project, grid=(4,), out_shape=jax.ShapeDtypeStruct(field.s...  5.01 us

profile of v4, /device:TPU:0, one launch (start us, length us, event | category | flops | bytes accessed | tf_op | source)
XLA Modules:
  0.0 45.8 jit_solution(11718349657440928037)
XLA Ops:
  0.0 40.8 %gather_and_factor.1 = (f32[4,4,32,2,8,128]{5,4,3,2,1,0:T(8,128)}, bf16[64,256]{1,0:T(8,128)(2,1)}) custom-call(f32[32,2,8,512]{3,2,1,0:T(8,128)} %field.1, f32[1,128]{1,0:T(1,128)} %bitcast.3, f32[32,128]{1,0:T(8,128)} %bitcast.2), custom_call_target="tpu_custom_call" | custom-call | tf_op jit(solution)/shard_map/gather_and_factor/pallas_call | solution.py:323
  40.8 5.0 %project.1 = f32[32,2,8,512]{3,2,1,0:T(8,128)} custom-call(bf16[64,256]{1,0:T(8,128)(2,1)} %get-tuple-element.7.weights_ref, f32[4,4,32,2,8,128]{5,4,3,2,1,0:T(8,128)} %get-tuple-element.8.field_ref), custom_call_target="tpu_custom_call" | custom-call | tf_op jit(solution)/shard_map/project/pallas_call | solution.py:351

commit v5 on v3

--- a/solution.py
+++ b/solution.py
@@ -114,11 +114,13 @@
     def lanes(j):
         return pl.ds(pl.multiple_of(j * 128, 128), 128)
 
-    local = []
-    for index, j in enumerate((me,) + others):
-        copy = pltpu.make_async_copy(field.at[:, :, :, lanes(j)], buf.at[j, me], local_sem.at[index])
-        copy.start()
-        local.append(copy)
+    local = {}
+    for a in range(2):
+        for index, j in ((2, peer), (3, cross), (1, sib), (0, me)):
+            copy = pltpu.make_async_copy(field.at[:, a, :, lanes(j)], buf.at[j, a, me],
+                                         local_sem.at[index, a])
+            copy.start()
+            local[index, a] = copy
 
     small = [pltpu.make_async_copy(gain_any, gain_ref, small_sem.at[0]),
              pltpu.make_async_copy(start_any, start_ref, small_sem.at[1])]
@@ -153,16 +155,20 @@
     for a in range(2):
         for rel in (1, 2, 0):
             other = others[rel]
-            copy = remote(field.at[:, a, :, lanes(other)], buf.at[other, me, :, a],
+            local[rel + 1, a].wait()
+            copy = remote(buf.at[other, a, me], buf.at[other, a, me],
                           send1.at[rel, a], recv1.at[rel, a], other)
             copy.start()
             first[rel, a] = copy
 
     second = []
     for index, j in enumerate((me, peer, cross)):
-        copy = remote(field.at[:, :, :, lanes(j)], buf.at[j, me], send2.at[index], recv2.at[index], sib)
-        copy.start()
-        second.append(copy)
+        for a in range(2):
+            if index == 0:
+                local[0, a].wait()
+            copy = remote(buf.at[j, a, me], buf.at[j, a, me], send2.at[index, a], recv2.at[index, a], sib)
+            copy.start()
+            second.append(copy)
 
     for copy in small:
         copy.wait()
@@ -171,21 +177,25 @@
     basis_t = start_ref[...]
 
     acc = jnp.zeros((256, 256), F32)
-    for copy in local:
-        copy.wait()
-    mine = buf.at[me].reshape(128 * rows, 128)
+    across = {}
     for a in range(2):
         for rel in range(3):
             first[rel, a].wait_recv()
+        if a == 1:
+            for piece in range(2):
+                for rel, j in ((1, me), (2, sib)):
+                    copy = remote(buf.at[j, piece, me], buf.at[j, piece, me], send3.at[rel - 1, piece],
+                                  recv3.at[rel - 1, piece], others[rel])
+                    copy.start()
+                    across[rel, piece] = copy
+        flat = buf.at[me, a].reshape(128 * layers, 128)
         for pair in range(layers // 2):
             block = []
             for l in (2 * pair, 2 * pair + 1):
-                x = mine[pl.ds(a * layers + l, 128, stride=rows), :]
-                hi, lo = split_two(x)
-                y = jnp.concatenate([hi, lo], axis=0)
+                y = above(*split_two(flat[pl.ds(l, 128, stride=layers), :]))
                 parts[me, a * layers + l] = y
                 block.append(y)
-            both = jnp.concatenate(block, axis=1)
+            both = beside(*block)
             acc = acc + lax.dot_general(both, both, (((1,), (1,)), ((), ())),
                                         preferred_element_type=F32)
     gram_part[...] = (acc[:128, :128] + acc[128:, 128:]) + (acc[:128, 128:] + acc[128:, :128])
@@ -210,7 +220,7 @@
                         rs_recv.at[rel], g, c)
         copy.start()
         scatter.append(copy)
-    relay_a = remote(buf.at[me, pl.ds(base, 2)], buf.at[me, pl.ds(base, 2)], relay_send.at[0],
+    relay_a = remote(buf.at[me, :, pl.ds(base, 2)], buf.at[me, :, pl.ds(base, 2)], relay_send.at[0],
                      relay_recv.at[0], sib)
     relay_a.start()
     for copy in scatter:
@@ -244,32 +254,21 @@
 
     lax.fori_loop(1, halves, start_broadcast, 0)
 
-    across = {}
-    for a in range(2):
-        for rel, j in ((1, me), (2, sib)):
-            across[rel, a] = remote(field.at[:, a, :, lanes(j)], buf.at[j, me, :, a],
-                                    send3.at[rel - 1, a], recv3.at[rel - 1, a], others[rel])
-
-    def start_across(a):
-        for rel in (1, 2):
-            across[rel, a].start()
-
     def relay_across(a):
         for rel in (1, 2):
             across[rel, a].wait_recv()
-        place = buf.at[peer, pl.ds(base, 2), :, a]
+        place = buf.at[peer, a, pl.ds(base, 2)]
         copy = remote(place, place, relay_send.at[1 + a], relay_recv.at[1 + a], sib)
         copy.start()
         return copy
 
-    start_across(0)
-
-    def prepare(j, g):
-        source = buf.at[j, g].reshape(own * rows, 128)
-        for r in range(rows):
-            hi, lo = split_two(source[pl.ds(r, own, stride=rows), :])
-            parts[j, r, own_rows(g), :] = hi
-            parts[j, r, pl.ds(pl.multiple_of(128 + g * own, own), own), :] = lo
+    def prepare(j, g, pieces=(0, 1)):
+        for a in pieces:
+            source = buf.at[j, a, g].reshape(own * layers, 128)
+            for l in range(layers):
+                hi, lo = split_two(source[pl.ds(l, own, stride=layers), :])
+                parts[j, a * layers + l, own_rows(g), :] = hi
+                parts[j, a * layers + l, pl.ds(pl.multiple_of(128 + g * own, own), own), :] = lo
 
     for j in (sib, peer, cross):
         prepare(j, me)
@@ -294,14 +293,16 @@
     for copy in gather:
         copy.wait_recv()
 
-    start_across(1)
     weights = gram_weights(gram_full[...] * gain_row * gain_col * (1.0 / total_rows))
     basis_t = refine_step(weights, basis_t)
     relay_a.wait_recv()
     for g in (peer, cross):
         prepare(sib, g)
     relays = [relay_across(0)]
-    for step in range(1, ITERS):
+    basis_t = refine_step(weights, basis_t)
+    for g in (peer, cross):
+        prepare(peer, g, (0,))
+    for step in range(2, ITERS):
         basis_t = refine_step(weights, basis_t)
     relays.append(relay_across(1))
     proj_ref[...] = outer_of(basis_t)
@@ -309,23 +310,29 @@
     weights = above(beside(hi, hi), beside(lo, jnp.zeros_like(lo)))
 
     for g in (peer, cross):
-        prepare(peer, g)
+        prepare(peer, g, (1,))
+    relays[0].wait_recv()
+    for g in (peer, cross):
+        prepare(cross, g, (0,))
     written = []
     for index, j in enumerate((me,) + others):
         if index == 3:
-            for copy in relays:
-                copy.wait_recv()
+            relays[1].wait_recv()
             for g in (peer, cross):
-                prepare(cross, g)
-        target = out_buf.at[j].reshape(own * rows, 128)
+                prepare(cross, g, (1,))
         for r in range(0, rows, 2):
+            target = out_buf.at[j, r // layers].reshape(own * layers, 128)
+            l = r % layers
             result = jnp.dot(weights, beside(parts[j, r], parts[j, r + 1]), preferred_element_type=F32)
             result = result[:own] + result[own:]
-            target[pl.ds(r, own, stride=rows), :] = result[:, :128]
-            target[pl.ds(r + 1, own, stride=rows), :] = result[:, 128:]
-        copy = pltpu.make_async_copy(out_buf.at[j], out.at[:, :, :, lanes(j)], out_sem.at[index])
-        copy.start()
-        written.append(copy)
+            target[pl.ds(l, own, stride=layers), :] = result[:, :128]
+            target[pl.ds(l + 1, own, stride=layers), :] = result[:, 128:]
+            if l + 2 == layers:
+                a = r // layers
+                copy = pltpu.make_async_copy(out_buf.at[j, a], out.at[:, a, :, lanes(j)],
+                                             out_sem.at[index, a])
+                copy.start()
+                written.append(copy)
 
     for copy in list(first.values()) + second + list(across.values()) + scatter + gather + [relay_a] + relays:
         copy.wait_send()
@@ -343,12 +350,12 @@
     return pl.pallas_call(
         functools.partial(kernel, cells, total_rows),
         out_shape=jax.ShapeDtypeStruct(field.shape, F32),
-        in_specs=[any_space, any_space, any_space],
+        in_specs=[pl.BlockSpec(memory_space=pltpu.HBM)] * 3,
         out_specs=any_space,
         scratch_shapes=[
-            pltpu.VMEM((4, 4, own, 2, layers, 128), F32),
+            pltpu.VMEM((4, 2, 4, own, layers, 128), F32),
             pltpu.VMEM((4, 2 * layers, 256, 128), BF16),
-            pltpu.VMEM((4, own, 2, layers, 128), F32),
+            pltpu.VMEM((4, 2, own, layers, 128), F32),
             pltpu.VMEM((1, 128), F32),
             pltpu.VMEM(start_basis.shape[::-1], F32),
             pltpu.VMEM((128, 128), F32),
@@ -356,9 +363,9 @@
             pltpu.VMEM((cells // 2, own // 2, 128), F32),
             pltpu.VMEM((128, 128), F32),
             pltpu.VMEM((128, 128), F32),
-            dma((4,)), dma((2,)), dma((4,)),
+            dma((4, 2)), dma((2,)), dma((4, 2)),
             dma((3, 2)), dma((3, 2)),
-            dma((3,)), dma((3,)),
+            dma((3, 2)), dma((3, 2)),
             dma((2, 2)), dma((2, 2)),
             dma((3,)), dma((3,)),
             dma((8,)), dma((8,)),
@@ -366,7 +373,7 @@
             dma((8,)), dma((8,)),
         ],
         compiler_params=pltpu.CompilerParams(
-            collective_id=0, has_side_effects=True, vmem_limit_bytes=56 * 1024 * 1024),
+            collective_id=0, has_side_effects=True, vmem_limit_bytes=36 * 1024 * 1024),
         name="factor_and_project",
     )(field, period_gain.reshape(1, -1), start_basis.T)
 

time: 42.9 us -> 50.8 us (1.18)
  Pallas kernels: 40.4 us -> 46.8 us
  local copies, waits for them, and re-layouts: 2.31 us -> 3.57 us
    pallas_call x1, Pallas kernels: 40.4 us -> 46.8 us  [per_device(): pl.pallas_call(functools.partial(kernel, cells, total_rows), out_shape=ja...]
    unnamed x1 -> x7, local copies, waits for them, and re-layouts: 2.31 us -> 3.57 us
where the time goes in v5:
time: 50.8 us; the launch traced here: 50.4 us
  Pallas kernels  46.8 us (92%)
  local copies, waits for them, and re-layouts  3.57 us (7%)
    pallas_call x1, Pallas kernels, per_device(): pl.pallas_call(functools.partial(kernel, cells, total_rows), out_shape=ja...  46.8 us
    unnamed x7, local copies, waits for them, and re-layouts  3.57 us

profile of v5, /device:TPU:0, one launch (start us, length us, event | category | flops | bytes accessed | tf_op | source)
XLA Modules:
  0.0 50.4 jit_solution(16385670641030131905)
XLA Ops:
  0.0 0.0 copy-start.2
  0.0 0.7 %copy-done.2 = f32[128]{0:T(128)S(1)} copy-done((f32[128]{0:T(128)S(1)}, f32[128]{0:T(128)}, u32[]{:S(2)}) %copy-start.2) | copy-done | bytes 536
  0.7 0.0 copy-start
  0.7 1.2 %copy-done = f32[32,2,8,512]{3,2,1,0:T(8,128)S(1)} copy-done((f32[32,2,8,512]{3,2,1,0:T(8,128)S(1)}, f32[32,2,8,512]{3,2,1,0:T(8,128)}, u32[]{:S(2)}) %copy-start) | copy-done | bytes 1048600
  1.9 0.0 copy-start.1
  1.9 0.7 %copy-done.1 = f32[128,32]{0,1:T(8,128)S(1)} copy-done((f32[128,32]{0,1:T(8,128)S(1)}, f32[128,32]{0,1:T(8,128)}, u32[]{:S(2)}) %copy-start.1) | copy-done | bytes 16408
  2.6 46.8 %factor_and_project.1 = f32[32,2,8,512]{3,2,1,0:T(8,128)S(1)} custom-call(f32[32,2,8,512]{3,2,1,0:T(8,128)S(1)} %copy-done, f32[1,128]{1,0:T(1,128)S(1)} %bitcast.3, f32[32,128]{1,0:T(8,128)S(1)} %bitcast.2), custom_call_target="tpu_custom_call" | custom-call | tf_op jit(solution)/shard_map/factor_and_project/pallas_call | solution.py:350
  49.4 1.0 %copy.5 = f32[32,2,8,512]{3,2,1,0:T(8,128)} copy(f32[32,2,8,512]{3,2,1,0:T(8,128)S(1)} %factor_and_project.1) | data formatting | bytes 2097152
Async XLA Ops:
  0.0 0.7 %copy-start.2 = (f32[128]{0:T(128)S(1)}, f32[128]{0:T(128)}, u32[]{:S(2)}) copy-start(f32[128]{0:T(128)} %param.4) | copy-start | bytes 1540
  0.7 1.2 %copy-start = (f32[32,2,8,512]{3,2,1,0:T(8,128)S(1)}, f32[32,2,8,512]{3,2,1,0:T(8,128)}, u32[]{:S(2)}) copy-start(f32[32,2,8,512]{3,2,1,0:T(8,128)} %field.1) | copy-start | bytes 3145732
  1.9 0.7 %copy-start.1 = (f32[128,32]{0,1:T(8,128)S(1)}, f32[128,32]{0,1:T(8,128)}, u32[]{:S(2)}) copy-start(f32[128,32]{0,1:T(8,128)} %param.5) | copy-start | bytes 49156

commit v6 on v5

--- a/solution.py
+++ b/solution.py
@@ -177,17 +177,9 @@
     basis_t = start_ref[...]
 
     acc = jnp.zeros((256, 256), F32)
-    across = {}
     for a in range(2):
         for rel in range(3):
             first[rel, a].wait_recv()
-        if a == 1:
-            for piece in range(2):
-                for rel, j in ((1, me), (2, sib)):
-                    copy = remote(buf.at[j, piece, me], buf.at[j, piece, me], send3.at[rel - 1, piece],
-                                  recv3.at[rel - 1, piece], others[rel])
-                    copy.start()
-                    across[rel, piece] = copy
         flat = buf.at[me, a].reshape(128 * layers, 128)
         for pair in range(layers // 2):
             block = []
@@ -254,13 +246,27 @@
 
     lax.fori_loop(1, halves, start_broadcast, 0)
 
-    def relay_across(a):
+    pieces = ((0, 0, own // 2), (0, own // 2, own // 2), (1, 0, own))
+    across = {}
+    for n, (a, first_row, count) in enumerate(pieces):
+        for rel, j in ((1, me), (2, sib)):
+            place = buf.at[j, a, me, pl.ds(first_row, count)]
+            across[rel, n] = remote(place, place, send3.at[rel - 1, n], recv3.at[rel - 1, n], others[rel])
+
+    def start_across(n):
         for rel in (1, 2):
-            across[rel, a].wait_recv()
-        place = buf.at[peer, a, pl.ds(base, 2)]
-        copy = remote(place, place, relay_send.at[1 + a], relay_recv.at[1 + a], sib)
+            across[rel, n].start()
+
+    def relay_across(n):
+        for rel in (1, 2):
+            across[rel, n].wait_recv()
+        a, first_row, count = pieces[n]
+        place = buf.at[peer, a, pl.ds(base, 2), pl.ds(first_row, count)]
+        copy = remote(place, place, relay_send.at[1 + n], relay_recv.at[1 + n], sib)
         copy.start()
         return copy
+
+    start_across(0)
 
     def prepare(j, g, pieces=(0, 1)):
         for a in pieces:
@@ -290,6 +296,8 @@
                         ag_recv.at[rel], g, c)
         copy.start()
         gather.append(copy)
+    start_across(1)
+    start_across(2)
     for copy in gather:
         copy.wait_recv()
 
@@ -300,26 +308,26 @@
         prepare(sib, g)
     relays = [relay_across(0)]
     basis_t = refine_step(weights, basis_t)
+    relays.append(relay_across(1))
     for g in (peer, cross):
         prepare(peer, g, (0,))
     for step in range(2, ITERS):
         basis_t = refine_step(weights, basis_t)
-    relays.append(relay_across(1))
     proj_ref[...] = outer_of(basis_t)
     hi, lo = split_two(proj_ref[own_rows(me), :] * gain_row)
     weights = above(beside(hi, hi), beside(lo, jnp.zeros_like(lo)))
 
-    for g in (peer, cross):
-        prepare(peer, g, (1,))
-    relays[0].wait_recv()
-    for g in (peer, cross):
-        prepare(cross, g, (0,))
     written = []
     for index, j in enumerate((me,) + others):
+        if index == 2:
+            relays.append(relay_across(2))
+            for g in (peer, cross):
+                prepare(peer, g, (1,))
         if index == 3:
-            relays[1].wait_recv()
+            for copy in relays:
+                copy.wait_recv()
             for g in (peer, cross):
-                prepare(cross, g, (1,))
+                prepare(cross, g)
         for r in range(0, rows, 2):
             target = out_buf.at[j, r // layers].reshape(own * layers, 128)
             l = r % layers
@@ -341,16 +349,26 @@
         copy.wait()
 
 
+def hand_over(source, target, sems):
+    count = source.shape[0] // 8
+    copies = [pltpu.make_async_copy(source.at[pl.ds(i * count, count)], target.at[pl.ds(i * count, count)],
+                                    sems.at[i]) for i in range(8)]
+    for copy in copies:
+        copy.start()
+    for copy in copies:
+        copy.wait()
+
+
 def per_device(field, period_gain, start_basis):
     cells = lax.axis_size("cells")
     own, _, layers, width = field.shape
     total_rows = 2.0 * layers * width * cells
     any_space = pl.BlockSpec(memory_space=pl.ANY)
     dma = pltpu.SemaphoreType.DMA
-    return pl.pallas_call(
+    result = pl.pallas_call(
         functools.partial(kernel, cells, total_rows),
         out_shape=jax.ShapeDtypeStruct(field.shape, F32),
-        in_specs=[pl.BlockSpec(memory_space=pltpu.HBM)] * 3,
+        in_specs=[any_space] * 3,
         out_specs=any_space,
         scratch_shapes=[
             pltpu.VMEM((4, 2, 4, own, layers, 128), F32),
@@ -366,16 +384,25 @@
             dma((4, 2)), dma((2,)), dma((4, 2)),
             dma((3, 2)), dma((3, 2)),
             dma((3, 2)), dma((3, 2)),
-            dma((2, 2)), dma((2, 2)),
-            dma((3,)), dma((3,)),
+            dma((2, 3)), dma((2, 3)),
+            dma((4,)), dma((4,)),
             dma((8,)), dma((8,)),
             dma((cells // 2,)), dma((cells // 2,)),
             dma((8,)), dma((8,)),
         ],
         compiler_params=pltpu.CompilerParams(
-            collective_id=0, has_side_effects=True, vmem_limit_bytes=36 * 1024 * 1024),
+            collective_id=0, has_side_effects=True, vmem_limit_bytes=56 * 1024 * 1024),
         name="factor_and_project",
     )(field, period_gain.reshape(1, -1), start_basis.T)
+    return pl.pallas_call(
+        hand_over,
+        out_shape=jax.ShapeDtypeStruct(field.shape, F32),
+        in_specs=[any_space],
+        out_specs=any_space,
+        scratch_shapes=[dma((8,))],
+        compiler_params=pltpu.CompilerParams(vmem_limit_bytes=56 * 1024 * 1024),
+        name="hand_over",
+    )(result)
 
 
 def solution(mesh):

time: 50.8 us -> 71.1 us (1.40)
  Pallas kernels: 46.8 us -> 70.9 us
  local copies, waits for them, and re-layouts: 3.57 us -> 0 us
    pallas_call x0 -> x1, Pallas kernels: none -> 32.9 us  [per_device(): pl.pallas_call(hand_over, out_shape=jax.ShapeDtypeStruct(field.shape, F32...]
    pallas_call x1, Pallas kernels: 46.8 us -> 38 us  [per_device(): pl.pallas_call(functools.partial(kernel, cells, total_rows), out_shape=ja...]
    unnamed x7 -> x0, local copies, waits for them, and re-layouts: 3.57 us -> none
where the time goes in v6:
time: 71.1 us; the launch traced here: 70.9 us
  Pallas kernels  70.9 us (100%)
    pallas_call x1, Pallas kernels, per_device(): pl.pallas_call(functools.partial(kernel, cells, total_rows), out_shape=ja...  38 us
    pallas_call x1, Pallas kernels, per_device(): pl.pallas_call(hand_over, out_shape=jax.ShapeDtypeStruct(field.shape, F32...  32.9 us

profile of v6, /device:TPU:0, one launch (start us, length us, event | category | flops | bytes accessed | tf_op | source)
XLA Modules:
  0.0 70.9 jit_solution(10093425282129024440)
XLA Ops:
  0.0 38.0 %factor_and_project.1.source = f32[32,2,8,512]{3,2,1,0:T(8,128)} custom-call(f32[32,2,8,512]{3,2,1,0:T(8,128)} %field.1, f32[1,128]{1,0:T(1,128)} %bitcast.3, f32[32,128]{1,0:T(8,128)} %bitcast.2), custom_call_target="tpu_custom_call" | custom-call | tf_op jit(solution)/shard_map/factor_and_project/pallas_call | solution.py:368
  38.0 32.9 %hand_over.1 = f32[32,2,8,512]{3,2,1,0:T(8,128)} custom-call(f32[32,2,8,512]{3,2,1,0:T(8,128)} %factor_and_project.1.source), custom_call_target="tpu_custom_call" | custom-call | tf_op jit(solution)/shard_map/hand_over/pallas_call | solution.py:397

commit v7 on v6

--- a/solution.py
+++ b/solution.py
@@ -161,11 +161,27 @@
             copy.start()
             first[rel, a] = copy
 
+    for a in range(2):
+        local[0, a].wait()
+
+    half_own, eighth = own // 2, own // 8
+    pieces = ((0, 0, eighth), (0, eighth, half_own - eighth), (0, half_own, half_own),
+              (1, 0, half_own), (1, half_own, half_own))
+    across = {}
+    for n, (a, first_row, count) in enumerate(pieces):
+        for rel, j in ((1, me), (2, sib)):
+            place = buf.at[j, a, me, pl.ds(first_row, count)]
+            across[rel, n] = remote(place, place, send3.at[rel - 1, n], recv3.at[rel - 1, n], others[rel])
+
+    def start_across(n):
+        for rel in (1, 2):
+            across[rel, n].start()
+
+    start_across(0)
+
     second = []
     for index, j in enumerate((me, peer, cross)):
         for a in range(2):
-            if index == 0:
-                local[0, a].wait()
             copy = remote(buf.at[j, a, me], buf.at[j, a, me], send2.at[index, a], recv2.at[index, a], sib)
             copy.start()
             second.append(copy)
@@ -246,27 +262,18 @@
 
     lax.fori_loop(1, halves, start_broadcast, 0)
 
-    pieces = ((0, 0, own // 2), (0, own // 2, own // 2), (1, 0, own))
-    across = {}
-    for n, (a, first_row, count) in enumerate(pieces):
-        for rel, j in ((1, me), (2, sib)):
-            place = buf.at[j, a, me, pl.ds(first_row, count)]
-            across[rel, n] = remote(place, place, send3.at[rel - 1, n], recv3.at[rel - 1, n], others[rel])
-
-    def start_across(n):
-        for rel in (1, 2):
-            across[rel, n].start()
-
-    def relay_across(n):
-        for rel in (1, 2):
-            across[rel, n].wait_recv()
-        a, first_row, count = pieces[n]
+    def relay_across(n, *received):
+        for m in received:
+            for rel in (1, 2):
+                across[rel, m].wait_recv()
+        a, first_row = pieces[received[0]][:2]
+        count = sum(pieces[m][2] for m in received)
         place = buf.at[peer, a, pl.ds(base, 2), pl.ds(first_row, count)]
         copy = remote(place, place, relay_send.at[1 + n], relay_recv.at[1 + n], sib)
         copy.start()
         return copy
 
-    start_across(0)
+    start_across(1)
 
     def prepare(j, g, pieces=(0, 1)):
         for a in pieces:
@@ -296,8 +303,8 @@
                         ag_recv.at[rel], g, c)
         copy.start()
         gather.append(copy)
-    start_across(1)
-    start_across(2)
+    for n in (2, 3, 4):
+        start_across(n)
     for copy in gather:
         copy.wait_recv()
 
@@ -306,13 +313,14 @@
     relay_a.wait_recv()
     for g in (peer, cross):
         prepare(sib, g)
-    relays = [relay_across(0)]
+    relays = [relay_across(0, 0, 1)]
     basis_t = refine_step(weights, basis_t)
-    relays.append(relay_across(1))
+    relays.append(relay_across(1, 2))
     for g in (peer, cross):
         prepare(peer, g, (0,))
     for step in range(2, ITERS):
         basis_t = refine_step(weights, basis_t)
+    relays.append(relay_across(2, 3))
     proj_ref[...] = outer_of(basis_t)
     hi, lo = split_two(proj_ref[own_rows(me), :] * gain_row)
     weights = above(beside(hi, hi), beside(lo, jnp.zeros_like(lo)))
@@ -320,7 +328,7 @@
     written = []
     for index, j in enumerate((me,) + others):
         if index == 2:
-            relays.append(relay_across(2))
+            relays.append(relay_across(3, 4))
             for g in (peer, cross):
                 prepare(peer, g, (1,))
         if index == 3:
@@ -349,13 +357,19 @@
         copy.wait()
 
 
-def hand_over(source, target, sems):
+def hand_over(source, target, block, sems):
     count = source.shape[0] // 8
-    copies = [pltpu.make_async_copy(source.at[pl.ds(i * count, count)], target.at[pl.ds(i * count, count)],
-                                    sems.at[i]) for i in range(8)]
-    for copy in copies:
+    places = [pl.ds(i * count, count) for i in range(8)]
+    loads = [pltpu.make_async_copy(source.at[place], block.at[place], sems.at[0, i])
+             for i, place in enumerate(places)]
+    stores = [pltpu.make_async_copy(block.at[place], target.at[place], sems.at[1, i])
+              for i, place in enumerate(places)]
+    for copy in loads:
         copy.start()
-    for copy in copies:
+    for load, store in zip(loads, stores):
+        load.wait()
+        store.start()
+    for copy in stores:
         copy.wait()
 
 
@@ -384,8 +398,8 @@
             dma((4, 2)), dma((2,)), dma((4, 2)),
             dma((3, 2)), dma((3, 2)),
             dma((3, 2)), dma((3, 2)),
-            dma((2, 3)), dma((2, 3)),
-            dma((4,)), dma((4,)),
+            dma((2, 5)), dma((2, 5)),
+            dma((5,)), dma((5,)),
             dma((8,)), dma((8,)),
             dma((cells // 2,)), dma((cells // 2,)),
             dma((8,)), dma((8,)),
@@ -399,7 +413,7 @@
         out_shape=jax.ShapeDtypeStruct(field.shape, F32),
         in_specs=[any_space],
         out_specs=any_space,
-        scratch_shapes=[dma((8,))],
+        scratch_shapes=[pltpu.VMEM(field.shape, F32), dma((2, 8))],
         compiler_params=pltpu.CompilerParams(vmem_limit_bytes=56 * 1024 * 1024),
         name="hand_over",
     )(result)

time: 71.1 us -> 40.1 us (0.56)
  Pallas kernels: 70.9 us -> 40 us
    pallas_call x1, Pallas kernels: 32.9 us -> 2.09 us  [per_device(): pl.pallas_call(hand_over, out_shape=jax.ShapeDtypeStruct(field.shape, F32...]
where the time goes in v7:
time: 40.1 us; the launch traced here: 40 us
  Pallas kernels  40 us (100%)
    pallas_call x1, Pallas kernels, per_device(): pl.pallas_call(functools.partial(kernel, cells, total_rows), out_shape=ja...  37.9 us
    pallas_call x1, Pallas kernels, per_device(): pl.pallas_call(hand_over, out_shape=jax.ShapeDtypeStruct(field.shape, F32...  2.09 us

profile of v7, /device:TPU:0, one launch (start us, length us, event | category | flops | bytes accessed | tf_op | source)
XLA Modules:
  0.0 40.0 jit_solution(5455367488664838095)
XLA Ops:
  0.0 37.9 %factor_and_project.1.source = f32[32,2,8,512]{3,2,1,0:T(8,128)} custom-call(f32[32,2,8,512]{3,2,1,0:T(8,128)} %field.1, f32[1,128]{1,0:T(1,128)} %bitcast.3, f32[32,128]{1,0:T(8,128)} %bitcast.2), custom_call_target="tpu_custom_call" | custom-call | tf_op jit(solution)/shard_map/factor_and_project/pallas_call | solution.py:382
  37.9 2.1 %hand_over.1 = f32[32,2,8,512]{3,2,1,0:T(8,128)} custom-call(f32[32,2,8,512]{3,2,1,0:T(8,128)} %factor_and_project.1.source), custom_call_target="tpu_custom_call" | custom-call | tf_op jit(solution)/shard_map/hand_over/pallas_call | solution.py:411

commit v8 on v7

--- a/solution.py
+++ b/solution.py
@@ -192,8 +192,26 @@
     gain_col = jnp.broadcast_to(gain_row, (128, 128)).T
     basis_t = start_ref[...]
 
+    def own_rows(g):
+        return pl.ds(pl.multiple_of(g * own, own), own)
+
+    def prepare(j, g, pieces=(0, 1)):
+        for a in pieces:
+            source = buf.at[j, a, g].reshape(own * layers, 128)
+            for l in range(layers):
+                hi, lo = split_two(source[pl.ds(l, own, stride=layers), :])
+                parts[j, a * layers + l, own_rows(g), :] = hi
+                parts[j, a * layers + l, pl.ds(pl.multiple_of(128 + g * own, own), own), :] = lo
+
+    for j in (sib, peer, cross):
+        prepare(j, me)
     acc = jnp.zeros((256, 256), F32)
     for a in range(2):
+        if a == 1:
+            for copy in second:
+                copy.wait_recv()
+            for j in (sib, peer, cross):
+                prepare(j, sib)
         for rel in range(3):
             first[rel, a].wait_recv()
         flat = buf.at[me, a].reshape(128 * layers, 128)
@@ -208,9 +226,6 @@
                                         preferred_element_type=F32)
     gram_part[...] = (acc[:128, :128] + acc[128:, 128:]) + (acc[:128, 128:] + acc[128:, :128])
 
-    def own_rows(g):
-        return pl.ds(pl.multiple_of(g * own, own), own)
-
     def share(g, c):
         return pl.ds(pl.multiple_of((lax.rem(c, 2) * 4 + g) * (own // 2), own // 2), own // 2)
 
@@ -228,9 +243,6 @@
                         rs_recv.at[rel], g, c)
         copy.start()
         scatter.append(copy)
-    relay_a = remote(buf.at[me, :, pl.ds(base, 2)], buf.at[me, :, pl.ds(base, 2)], relay_send.at[0],
-                     relay_recv.at[0], sib)
-    relay_a.start()
     for copy in scatter:
         copy.wait_recv()
     slots[half] = ((gram_part[mine_only, :] + scattered[1]) + (scattered[2] + scattered[3])) + (
@@ -261,6 +273,9 @@
         return carry
 
     lax.fori_loop(1, halves, start_broadcast, 0)
+    relay_a = remote(buf.at[me, :, pl.ds(base, 2)], buf.at[me, :, pl.ds(base, 2)], relay_send.at[0],
+                     relay_recv.at[0], sib)
+    relay_a.start()
 
     def relay_across(n, *received):
         for m in received:
@@ -275,21 +290,6 @@
 
     start_across(1)
 
-    def prepare(j, g, pieces=(0, 1)):
-        for a in pieces:
-            source = buf.at[j, a, g].reshape(own * layers, 128)
-            for l in range(layers):
-                hi, lo = split_two(source[pl.ds(l, own, stride=layers), :])
-                parts[j, a * layers + l, own_rows(g), :] = hi
-                parts[j, a * layers + l, pl.ds(pl.multiple_of(128 + g * own, own), own), :] = lo
-
-    for j in (sib, peer, cross):
-        prepare(j, me)
-    for copy in second:
-        copy.wait_recv()
-    for j in (sib, peer, cross):
-        prepare(j, sib)
-
     lax.fori_loop(1, halves, wait_broadcast, 0)
 
     def add(step, total):
@@ -305,14 +305,14 @@
         gather.append(copy)
     for n in (2, 3, 4):
         start_across(n)
-    for copy in gather:
-        copy.wait_recv()
-
-    weights = gram_weights(gram_full[...] * gain_row * gain_col * (1.0 / total_rows))
-    basis_t = refine_step(weights, basis_t)
     relay_a.wait_recv()
     for g in (peer, cross):
         prepare(sib, g)
+    for copy in gather:
+        copy.wait_recv()
+
+    weights = gram_weights(gram_full[...] * gain_row * gain_col * (1.0 / total_rows))
+    basis_t = refine_step(weights, basis_t)
     relays = [relay_across(0, 0, 1)]
     basis_t = refine_step(weights, basis_t)
     relays.append(relay_across(1, 2))

time: 40.1 us -> 40.1 us (level)
  no operation moved by 1% of the time
where the time goes in v8:
time: 40.1 us; the launch traced here: 40 us
  Pallas kernels  40 us (100%)
    pallas_call x1, Pallas kernels, per_device(): pl.pallas_call(functools.partial(kernel, cells, total_rows), out_shape=ja...  37.9 us
    pallas_call x1, Pallas kernels, per_device(): pl.pallas_call(hand_over, out_shape=jax.ShapeDtypeStruct(field.shape, F32...  2.09 us

profile of v8, /device:TPU:0, one launch (start us, length us, event | category | flops | bytes accessed | tf_op | source)
XLA Modules:
  0.0 40.0 jit_solution(9209497694287776034)
XLA Ops:
  0.0 37.9 %factor_and_project.1.source = f32[32,2,8,512]{3,2,1,0:T(8,128)} custom-call(f32[32,2,8,512]{3,2,1,0:T(8,128)} %field.1, f32[1,128]{1,0:T(1,128)} %bitcast.3, f32[32,128]{1,0:T(8,128)} %bitcast.2), custom_call_target="tpu_custom_call" | custom-call | tf_op jit(solution)/shard_map/factor_and_project/pallas_call | solution.py:382
  37.9 2.1 %hand_over.1 = f32[32,2,8,512]{3,2,1,0:T(8,128)} custom-call(f32[32,2,8,512]{3,2,1,0:T(8,128)} %factor_and_project.1.source), custom_call_target="tpu_custom_call" | custom-call | tf_op jit(solution)/shard_map/hand_over/pallas_call | solution.py:411

commit v9 on v8

--- a/solution.py
+++ b/solution.py
@@ -165,7 +165,7 @@
         local[0, a].wait()
 
     half_own, eighth = own // 2, own // 8
-    pieces = ((0, 0, eighth), (0, eighth, half_own - eighth), (0, half_own, half_own),
+    pieces = ((0, 0, eighth), (0, eighth, 5 * eighth), (0, 6 * eighth, 2 * eighth),
               (1, 0, half_own), (1, half_own, half_own))
     across = {}
     for n, (a, first_row, count) in enumerate(pieces):

time: 40.1 us -> 39.7 us (0.990)
    pallas_call x1, Pallas kernels: 37.9 us -> 37.5 us  [per_device(): pl.pallas_call(functools.partial(kernel, cells, total_rows), out_shape=ja...]
where the time goes in v9:
time: 39.7 us; the launch traced here: 39.6 us
  Pallas kernels  39.6 us (100%)
    pallas_call x1, Pallas kernels, per_device(): pl.pallas_call(functools.partial(kernel, cells, total_rows), out_shape=ja...  37.5 us
    pallas_call x1, Pallas kernels, per_device(): pl.pallas_call(hand_over, out_shape=jax.ShapeDtypeStruct(field.shape, F32...  2.09 us

profile of v9, /device:TPU:0, one launch (start us, length us, event | category | flops | bytes accessed | tf_op | source)
XLA Modules:
  0.0 39.6 jit_solution(14337895538600876844)
XLA Ops:
  0.0 37.5 %factor_and_project.1.source = f32[32,2,8,512]{3,2,1,0:T(8,128)} custom-call(f32[32,2,8,512]{3,2,1,0:T(8,128)} %field.1, f32[1,128]{1,0:T(1,128)} %bitcast.3, f32[32,128]{1,0:T(8,128)} %bitcast.2), custom_call_target="tpu_custom_call" | custom-call | tf_op jit(solution)/shard_map/factor_and_project/pallas_call | solution.py:382
  37.5 2.1 %hand_over.1 = f32[32,2,8,512]{3,2,1,0:T(8,128)} custom-call(f32[32,2,8,512]{3,2,1,0:T(8,128)} %factor_and_project.1.source), custom_call_target="tpu_custom_call" | custom-call | tf_op jit(solution)/shard_map/hand_over/pallas_call | solution.py:411
